TPU v7x, 32 devices: a whole 2x2x4 slice. The times are simulated.
32 devices in a mesh: fsdp: 8 (over z, x), rep: 4 (over y, core).
Axes of the slice: x: 2, y: 2, z: 4, core: 2. Of those that a mesh axis runs over, the one named last changes fastest.
Arguments:
- inputs: bfloat16 [32, 512, 768], P(('fsdp', 'rep')), may hold values from -6 to 6
- lengths: int32 [32], P(('fsdp', 'rep')), may hold values from 128 to 512, as said below
- cotangent: bfloat16 [32, 512, 768], P(('fsdp', 'rep')), may hold values from -6 to 6
- query_weight: bfloat16 [768, 768], P('fsdp'), may hold values from -0.02734375 to 0.02734375
- key_weight: bfloat16 [768, 768], P('fsdp'), may hold values from -0.21875 to 0.21875
- value_weight: bfloat16 [768, 768], P('fsdp'), may hold values from -0.21875 to 0.21875
- output_weight: bfloat16 [768, 768], P('fsdp'), may hold values from -6 to 6
- attention_gain: bfloat16 [768], P('fsdp'), may hold values from 0.099609375 to 1.8984375
- bias_table: bfloat16 [32, 12], P('fsdp'), may hold values from -4 to 4
- inner_weight: bfloat16 [768, 3072], P('fsdp'), may hold values from -0.21875 to 0.21875
- outer_weight: bfloat16 [3072, 768], P('fsdp'), may hold values from -0.109375 to 0.109375
- feedforward_gain: bfloat16 [768], P('fsdp'), may hold values from 0.099609375 to 1.8984375
Outputs:
- block_output: bfloat16 [32, 512, 768], P(('fsdp', 'rep'))
- input_grad: float32 [32, 512, 768], P(('fsdp', 'rep'))
- query_grad: float32 [768, 768], P('fsdp')
- key_grad: float32 [768, 768], P('fsdp')
- value_grad: float32 [768, 768], P('fsdp')
- output_grad: float32 [768, 768], P('fsdp')
- attention_gain_grad: float32 [768], P('fsdp')
- bias_table_grad: float32 [32, 12], P('fsdp')
- inner_grad: float32 [768, 3072], P('fsdp')
- outer_grad: float32 [3072, 768], P('fsdp')
- feedforward_gain_grad: float32 [768], P('fsdp')
Inputs may be any that keep to these rules, and one draw needn't show every extreme that they name: `lengths`: positions below a pair's entry hold the pair, the rest of its 512 slots is padding; some pair has exactly 512 and some exactly 128.
All inputs are finite; a program needn't handle non-finite values.
Results may differ from a plain program's by a relative error of at most 0.02.
Values may be sent and summed in bfloat16 or wider, within the bound.
A program may use at most 192 MiB of HBM per device.

v0:
```python
import functools

import jax
import jax.numpy as jnp
from jax import lax
import jax.experimental.pallas as pl
import jax.experimental.pallas.tpu as pltpu
from jax.sharding import PartitionSpec as P

NB = 32


epsilon = 1e-06
highest = lax.Precision.HIGHEST
gelu_coeff = 0.7978845608028654
masked_score = -1e30


def bucket_of(offset):
    half_count = NB // 2
    exact_count = half_count // 2
    distance = jnp.abs(offset)
    beyond = jnp.full(offset.shape, exact_count, jnp.int32)
    for exponent in range(1, half_count - exact_count):
        beyond = beyond + (distance * distance >= exact_count * exact_count * 2**exponent).astype(
            jnp.int32
        )
    nearby = jnp.where(distance < exact_count, distance, beyond)
    return jnp.where(offset > 0, half_count, 0).astype(jnp.int32) + nearby


def rms_norm(values, gain_vector):
    inverse_rms = lax.rsqrt(jnp.mean(values * values, axis=-1, keepdims=True) + epsilon)
    return values * inverse_rms * gain_vector


def gelu(values):
    return (
        0.5 * values * (1.0 + jnp.tanh(gelu_coeff * (values + 0.044715 * values * values * values)))
    )


def dot(a,b): return jnp.dot(a,b,preferred_element_type=jnp.float32)
def dot_t(a,b): return lax.dot_general(a,b,(((1,),(1,)),((),())),preferred_element_type=jnp.float32)
def dot_c(a,b): return lax.dot_general(a,b,(((0,),(0,)),((),())),preferred_element_type=jnp.float32)

def fwd_kernel(T, len_ref, q_ref, k_ref, v_ref, rel_ref, o_ref, p_ref, strip):
    hp=pl.program_id(0)
    seq=q_ref.shape[0]; nb=seq//T
    lane=lax.broadcasted_iota(jnp.int32,(1,128),1)
    kcol=lax.broadcasted_iota(jnp.int32,(1,seq),1)
    mask=jnp.where(kcol<len_ref[0],0.0,-1e30)
    k=k_ref[...]; v=v_ref[...]
    for hh in range(2):
        mine=(lane>=64) if hh else (lane<64)
        rel=rel_ref[pl.ds(hh,1),:]
        W=4*T
        rolled=pltpu.roll(jnp.broadcast_to(rel,(T,W)),0,axis=1,stride=1,stride_axis=0)
        strip[:, 2*T:5*T]=rolled[:, :3*T]
        far_neg=rel[:, 0:1]; far_pos=rel[:, 3*T-1:3*T]
        strip[:, 0:2*T]=jnp.broadcast_to(far_neg,(T,2*T))
        strip[:, 5*T:7*T]=jnp.broadcast_to(far_pos,(T,2*T))
        for I in range(nb):
            q=jnp.where(mine,q_ref[I*T:(I+1)*T,:],jnp.bfloat16(0))
            s=dot_t(q,k)+(strip[:, (3-I)*T:(3-I)*T+seq]+mask)
            m=jnp.max(s,axis=-1,keepdims=True)
            e=jnp.exp(s-m)
            tot=jnp.sum(e,axis=-1,keepdims=True)
            p=(e*(1.0/tot)).astype(jnp.bfloat16)
            p_ref[hh,I*T:(I+1)*T,:]=p
            o=dot(p,v)
            if hh==0:
                o_ref[I*T:(I+1)*T,:]=o.astype(jnp.bfloat16)
            else:
                o_ref[I*T:(I+1)*T,:]=jnp.where(mine,o.astype(jnp.bfloat16),o_ref[I*T:(I+1)*T,:])

def bwd_kernel(T, q_ref, k_ref, v_ref, do_ref, p_ref, dq_ref, dk_ref, dv_ref, db_ref, ds_ref):
    seq=q_ref.shape[0]; nb=seq//T
    lane=lax.broadcasted_iota(jnp.int32,(1,128),1)
    k=k_ref[...]; v=v_ref[...]
    dks=[];dvs=[]
    for hh in range(2):
        mine=(lane>=64) if hh else (lane<64)
        acc=[None]*5
        for I in range(nb):
            sl=slice(I*T,(I+1)*T)
            do=jnp.where(mine,do_ref[sl,:],jnp.bfloat16(0))
            dp=dot_t(do,v)
            p=p_ref[hh,sl,:].astype(jnp.float32)
            t=p*dp
            delta=jnp.sum(t,axis=-1,keepdims=True)
            ds=(t-p*delta).astype(jnp.bfloat16)
            ds_ref[sl,:]=ds
            dsf=ds.astype(jnp.float32)
            for J in range(nb):
                d=min(2,max(-2,J-I))+2
                x=dsf[:,J*T:(J+1)*T]
                acc[d]=x if acc[d] is None else acc[d]+x
            dq=dot(ds,k)
            if hh==0: dq_ref[sl,:]=dq.astype(jnp.bfloat16)
            else: dq_ref[sl,:]=jnp.where(mine,dq.astype(jnp.bfloat16),dq_ref[sl,:])
        near=jnp.concatenate([acc[1],acc[2],acc[3],jnp.zeros((T,T),jnp.float32)],axis=1)
        total=shear_sum(near,4*T)
        far=jnp.concatenate([jnp.zeros((1,2*T),jnp.float32),jnp.sum(acc[4],axis=0,keepdims=True),jnp.sum(acc[0],axis=0,keepdims=True)],axis=1)
        db_ref[hh:hh+1,:]=total+far
        dk=dot_c(q_ref[...],ds_ref[...]).T; dv=dot_c(do_ref[...],p_ref[hh]).T
        dks.append(dk); dvs.append(dv)
    dk_ref[...]=jnp.where(lane<64,dks[0],dks[1]).astype(jnp.bfloat16)
    dv_ref[...]=jnp.where(lane<64,dvs[0],dvs[1]).astype(jnp.bfloat16)

def rel_hits(tile):
    slot = jnp.arange(4 * tile, dtype=jnp.int32)
    offset = jnp.where(slot < 3 * tile, slot - tile, slot - 5 * tile)
    bucket_ids = jnp.arange(NB, dtype=jnp.int32)
    return (bucket_of(offset)[None, :] == bucket_ids[:, None]).astype(jnp.bfloat16)


def rel_vec(table, tile):
    return dot_c(table, rel_hits(tile))


def shear_sum(block, width):
    rows = block.shape[0]
    while rows > 8:
        rows //= 2
        block = block[:rows] + pltpu.roll(block[rows:], width - rows, axis=1)
    total = block[0:1]
    for r in range(1, 8):
        total = total + pltpu.roll(block[r : r + 1], width - r, axis=1)
    return total


def att_fwd(q,k,v,rel,length,T=128):
    seq,D=q.shape; H=rel.shape[0]
    blk=pl.BlockSpec((seq,128),lambda h: (0,h))
    return pl.pallas_call(functools.partial(fwd_kernel,T),grid=(H//2,),
        in_specs=[pl.BlockSpec(memory_space=pltpu.SMEM),blk,blk,blk,pl.BlockSpec((None,2,4*T),lambda h:(h,0,0))],
        out_specs=[blk,pl.BlockSpec((2,seq,seq),lambda h:(h,0,0))],
        out_shape=[jax.ShapeDtypeStruct((seq,D),jnp.bfloat16),jax.ShapeDtypeStruct((H,seq,seq),jnp.bfloat16)],
        scratch_shapes=[pltpu.VMEM((T,7*T),jnp.float32)],
        compiler_params=pltpu.CompilerParams(vmem_limit_bytes=40*2**20))(length,q,k,v,rel.reshape(H//2,2,4*T))
def att_bwd(q,k,v,do,p,T=128):
    seq,D=q.shape; H=p.shape[0]
    blk=pl.BlockSpec((seq,128),lambda h: (0,h))
    o=jax.ShapeDtypeStruct((seq,D),jnp.bfloat16)
    outs=pl.pallas_call(functools.partial(bwd_kernel,T),grid=(H//2,),
        in_specs=[blk,blk,blk,blk,pl.BlockSpec((2,seq,seq),lambda h:(h,0,0))],
        out_specs=[blk,blk,blk,pl.BlockSpec((None,2,4*T),lambda h:(h,0,0))],
        out_shape=[o,o,o,jax.ShapeDtypeStruct((H//2,2,4*T),jnp.float32)],
        scratch_shapes=[pltpu.VMEM((seq,seq),jnp.bfloat16)],
        compiler_params=pltpu.CompilerParams(vmem_limit_bytes=40*2**20))(q,k,v,do,p)
    return *outs[:3],outs[3].reshape(H,4*T)

def contract_rows(left, right):
    return lax.dot_general(
        left, right, (((0,), (0,)), ((), ())), preferred_element_type=jnp.float32
    )


def contract_cols(left, right):
    return lax.dot_general(
        left, right, (((1,), (1,)), ((), ())), preferred_element_type=jnp.float32
    )


MESH = pl.DeviceIdType.MESH


def coords():
    shard = lax.axis_index("fsdp")
    copy = lax.axis_index("rep")
    return shard // 2, shard % 2, copy // 2, copy % 2


def greet(peers, at_end):
    barrier = pltpu.get_barrier_semaphore()
    for peer in peers[:-1]:
        pl.semaphore_signal(barrier, inc=1, device_id=peer, device_id_type=MESH)

    def last():
        pl.semaphore_signal(barrier, inc=1, device_id=peers[-1], device_id_type=MESH)

    pl.when(~at_end)(last)


def all_greeted(peers, at_end):
    barrier = pltpu.get_barrier_semaphore()
    pl.semaphore_wait(barrier, jnp.where(at_end, len(peers) - 1, len(peers)))


class Links:
    def __init__(self, rows, send_sems, recv_sems):
        self.send_sems, self.recv_sems = send_sems, recv_sems
        self.z, self.x, self.y, self.c = coords()
        half = rows // 2
        part = half // 3
        at = lambda start, size: pl.ds(pl.multiple_of(start, part), size)
        first = half * self.c
        other = half * (1 - self.c)
        self.half, self.other_half = at(first, half), at(other, half)
        self.plane = at(first + part * self.y, 2 * part)
        self.shared = at(first + part, part)
        self.own_third = at(first + 2 * part * self.y, part)
        self.other_third = at(first + 2 * part * (1 - self.y), part)
        self.shared_in = at(part * self.y, part)
        self.third_in = at(part * (1 - self.y), part)

    def copy(self, src, dst, g, send, slot, device):
        return pltpu.make_async_remote_copy(
            src_ref=src,
            dst_ref=dst,
            send_sem=self.send_sems.at[send],
            recv_sem=self.recv_sems.at[g, slot],
            device_id=device,
            device_id_type=MESH,
        )

    def to_x(self):
        return (self.z * 2 + 1 - self.x, self.y * 2 + self.c)

    def to_y(self):
        return (self.z * 2 + self.x, (1 - self.y) * 2 + self.c)

    def to_core(self):
        return (self.z * 2 + self.x, self.y * 2 + 1 - self.c)

    def to_z(self, k):
        return (lax.rem(self.z + k, 4) * 2 + self.x, self.y * 2 + self.c)

    def z_before(self, k):
        return lax.rem(self.z + 4 - k, 4)


class Gather(Links):
    slots = 6

    def __init__(self, full, send_sems, recv_sems):
        super().__init__(full.shape[3], send_sems, recv_sems)
        self.full = full
        self.beside = self.z + 1 - 2 * lax.rem(self.z, 2)
        self.second = lax.rem(self.z + 2, 4)
        self.across = 3 - self.z
        self.at_end = (self.z == 0) | (self.z == 3)
        self.early = range(4, 8)

    def peers(self):
        near = [self.to_x(), self.to_y(), self.to_core()]
        return near + [self.at_z(a) for a in (self.second, self.beside, self.across)]

    def block(self, g, a, rows):
        return self.full.at[a, self.x, g, rows]

    def column(self, g, rows):
        return self.full.at[:, 1 - self.x, g, rows]

    def move(self, part, g, slot, device):
        return pltpu.make_async_remote_copy(
            src_ref=part,
            dst_ref=part,
            send_sem=self.send_sems.at[0 if g in self.early else 1],
            recv_sem=self.recv_sems.at[g, slot],
            device_id=device,
            device_id_type=MESH,
        )

    def at_z(self, a):
        return (a * 2 + self.x, self.y * 2 + self.c)

    def z_copy(self, g, to, slot):
        return self.move(self.block(g, self.z, self.plane), g, slot, self.at_z(to))

    def x_copy(self, g, a):
        return self.move(self.block(g, a, self.plane), g, 3, self.to_x())

    def y_copy(self, g, a):
        return self.move(self.block(g, a, self.own_third), g, 4, self.to_y())

    def core_copy(self, g, a):
        return self.move(self.block(g, a, self.half), g, 5, self.to_core())

    def arrived(self, part, g, slot):
        pltpu.make_async_copy(part, part, self.recv_sems.at[g, slot]).wait()

    def others(self):
        return (self.beside, self.second, self.across)

    def send_z(self, g):
        self.z_copy(g, self.second, 0).start()
        self.z_copy(g, self.beside, 1).start()
        pl.when(~self.at_end)(lambda: self.z_copy(g, self.across, 2).start())

    def send_x(self, g):
        self.x_copy(g, self.z).start()

    def spread(self, g, a, slot):
        self.arrived(self.block(g, a, self.plane), g, slot)
        if slot == 0:
            part = self.block(g, a, self.plane)
            pl.when(~self.at_end)(lambda: self.move(part, g, 2, self.at_z(self.beside)).start())
        self.x_copy(g, a).start()
        self.y_copy(g, a).start()

    def after_second(self, g):
        self.spread(g, self.second, 0)

    def after_beside(self, g):
        self.spread(g, self.beside, 1)

    def after_across(self, g):
        self.spread(g, self.across, 2)

    def after_x(self, g):
        self.arrived(self.column(g, self.plane), g, 3)
        self.move(self.column(g, self.own_third), g, 4, self.to_y()).start()

    def after_y(self, g):
        third = self.own_third.size
        self.arrived(self.full.at[0, 0, 0:7, 0:third], g, 4)
        for a in self.others():
            self.core_copy(g, a).start()
        self.move(self.column(g, self.half), g, 5, self.to_core()).start()

    def after_core(self, g):
        self.arrived(self.full.at[0, 0, 0:7, 0 : self.half.size], g, 5)

    def drain(self, n):
        count = len(self.early)
        units = self.full.shape[2] - 8
        rows = self.full.shape[3] * (count if n == 0 else units - count) // units

        def wait(blocks):
            part = self.full.at[:, :, 0:blocks, 0:rows]
            pltpu.make_async_copy(part, part, self.send_sems.at[n]).wait()

        pl.when(self.at_end)(lambda: wait(10))
        pl.when(~self.at_end)(lambda: wait(11))


class SmallGather(Gather):
    def move(self, part, g, slot, device):
        return pltpu.make_async_remote_copy(
            src_ref=part,
            dst_ref=part,
            send_sem=self.send_sems.at[0],
            recv_sem=self.recv_sems.at[slot],
            device_id=device,
            device_id_type=MESH,
        )

    def __init__(self, links, full, send_sems, recv_sems):
        self.__dict__.update(links.__dict__)
        self.full, self.send_sems, self.recv_sems = full, send_sems, recv_sems

    def block(self, g, a, rows):
        return self.full.at[a * 2 + self.x]

    def y_copy(self, g, a):
        return self

    def start(self):
        pass

    def arrived(self, part, g, slot):
        pltpu.make_async_copy(part, part, self.recv_sems.at[slot]).wait()

    def after_x(self, g):
        self.arrived(self.full.at[0:4], g, 3)

    def drain(self, n):
        def wait(blocks):
            part = self.full.at[0:blocks]
            pltpu.make_async_copy(part, part, self.send_sems.at[0]).wait()

        pl.when(self.at_end)(lambda: wait(6))
        pl.when(~self.at_end)(lambda: wait(8))


class Scatter(Links):
    slots = 6

    def __init__(self, slot, full, own, from_core, from_y, from_x, from_z, send_sems, recv_sems):
        super().__init__(own.shape[1], send_sems, recv_sems)
        self.slot, self.full, self.own = slot, full, own
        self.from_core, self.from_y, self.from_x, self.from_z = from_core, from_y, from_x, from_z

    def core_copy(self, g):
        part = self.full.at[:, :, self.slot(g), self.other_half]
        ring = g % self.from_core.shape[0]
        return self.copy(part, self.from_core.at[ring], g, 0, 0, self.to_core())

    def y_copy(self, g):
        part = self.full.at[:, :, self.slot(g), self.other_third]
        return self.copy(part, self.from_y.at[g], g, 1, 1, self.to_y())

    def x_copy(self, g):
        part = self.full.at[:, 1 - self.x, self.slot(g), self.plane]
        return self.copy(part, self.from_x.at[g], g, 1, 2, self.to_x())

    def z_copy(self, g, k):
        part = self.full.at[lax.rem(self.z + k, 4), self.x, self.slot(g), self.plane]
        return self.copy(part, self.from_z.at[g, k - 1], g, 2, 3, self.to_z(k))

    def back_y_copy(self, g):
        part = self.own.at[g, self.plane]
        return self.copy(part, self.from_z.at[g, 3], g, 4 + g, 4, self.to_y())

    def back_core_copy(self, g):
        part = self.own.at[g, self.half]
        return self.copy(part, part, g, 3, 5, self.to_core())

    def start(self, g):
        self.core_copy(g).start()

    def after_core(self, g):
        self.core_copy(g).wait_recv()
        ring = g % self.from_core.shape[0]
        for a in range(4):
            for b in range(2):
                self.full[a, b, self.slot(g), self.half] += self.from_core[ring, a, b]
        self.y_copy(g).start()

    def after_y(self, g):
        self.y_copy(g).wait_recv()
        for a in range(4):
            for b in range(2):
                self.full[a, b, self.slot(g), self.own_third] += self.from_y[g, a, b]
        self.x_copy(g).start()

    def after_x(self, g):
        self.x_copy(g).wait_recv()
        for a in range(4):
            self.full[a, self.x, self.slot(g), self.plane] += self.from_x[g, a]
        for k in (1, 2, 3):
            self.z_copy(g, k).start()

    def after_z(self, g):
        total = self.full[self.z, self.x, self.slot(g), self.plane].astype(jnp.float32)
        part = self.from_z.at[g, 0:3]
        pltpu.make_async_copy(part, part, self.recv_sems.at[g, 3]).wait()
        for k in (1, 2, 3):
            total = total + self.from_z[g, k - 1].astype(jnp.float32)
        self.own[g, self.plane] = total.astype(jnp.bfloat16)
        self.back_y_copy(g).start()

    def after_back_y(self, g):
        self.back_y_copy(g).wait_recv()
        self.back_y_copy(g).wait_send()
        got = self.from_z.at[g, 3]
        self.own[g, self.shared] += got[self.shared_in]
        self.own[g, self.other_third] = got[self.third_in]
        self.back_core_copy(g).start()

    def after_back_core(self, g):
        part = self.own.at[g, self.other_half]
        self.copy(part, part, g, 3, 5, self.to_core()).wait_recv()

    def drain(self):
        units, rows = self.own.shape[:2]
        half = rows // 2
        for n, part in (
            (0, self.full.at[:, :, 0 : units // 2]),
            (1, self.full.at[:, :, 0 : units // 3]),
            (2, self.full.at[:, :, 0 : units // 4, 0:half]),
            (3, self.own.at[0 : units // 2]),
        ):
            pltpu.make_async_copy(part, part, self.send_sems.at[n]).wait()


def compute(inputs, lengths, cotangent, weights):
    (
        full_query, full_key, full_value, full_output, full_gain, full_table, full_inner,
        full_outer, full_ffn_gain,
    ) = weights
    pairs_here, seq_len, model_width = inputs.shape
    row_count = pairs_here * seq_len
    head_count = full_table.shape[1]
    tile = 128
    relative = rel_vec(full_table, tile)
    flat_inputs = inputs.reshape(row_count, model_width).astype(jnp.float32)
    normed = rms_norm(flat_inputs, full_gain.astype(jnp.float32)).astype(jnp.bfloat16)
    joined = jnp.concatenate((full_query, full_key, full_value), axis=1)
    projected = jnp.dot(normed, joined, preferred_element_type=jnp.float32).astype(jnp.bfloat16)
    queries = projected[:, :model_width]
    key_rows = projected[:, model_width : 2 * model_width]
    value_rows = projected[:, 2 * model_width :]
    pair_rows = [slice(n * seq_len, (n + 1) * seq_len) for n in range(pairs_here)]
    forward_parts = [
        att_fwd(queries[r], key_rows[r], value_rows[r], relative, lengths[n : n + 1], tile)
        for n, r in enumerate(pair_rows)
    ]
    attended = jnp.concatenate([part[0] for part in forward_parts], axis=0)
    middle = flat_inputs + jnp.dot(attended, full_output, preferred_element_type=jnp.float32)
    normed_ffn = rms_norm(middle, full_ffn_gain.astype(jnp.float32)).astype(jnp.bfloat16)
    raised = jnp.dot(normed_ffn, full_inner, preferred_element_type=jnp.float32)
    active = gelu(raised).astype(jnp.bfloat16)
    lowered = jnp.dot(active, full_outer, preferred_element_type=jnp.float32)
    block_output = (middle + lowered).astype(jnp.bfloat16).reshape(pairs_here, seq_len, model_width)
    positions = jnp.arange(seq_len, dtype=jnp.int32)
    row_live = (positions[None, :] < lengths[:, None]).astype(jnp.float32)
    seed_rows = (cotangent.astype(jnp.float32) * row_live[:, :, None]).reshape(
        row_count, model_width
    )
    seed_low = seed_rows.astype(jnp.bfloat16)
    grad_active = contract_cols(seed_low, full_outer)
    grad_outer = contract_rows(active, seed_low)
    grad_raised = jax.vjp(gelu, raised)[1](grad_active)[0].astype(jnp.bfloat16)
    grad_inner = contract_rows(normed_ffn, grad_raised)
    grad_normed_ffn = contract_cols(grad_raised, full_inner)
    ffn_pull = jax.vjp(rms_norm, middle, full_ffn_gain.astype(jnp.float32))[1]
    grad_middle_part, grad_ffn_gain = ffn_pull(grad_normed_ffn)
    grad_middle = seed_rows + grad_middle_part
    joined = jnp.concatenate((full_query, full_key, full_value), axis=1)
    middle_low = grad_middle.astype(jnp.bfloat16)
    grad_attended = contract_cols(middle_low, full_output).astype(jnp.bfloat16)
    grad_output = contract_rows(attended, middle_low)
    backward_parts = [
        att_bwd(
            queries[r], key_rows[r], value_rows[r], grad_attended[r], forward_parts[n][1], tile
        )
        for n, r in enumerate(pair_rows)
    ]
    grad_projected = jnp.concatenate(
        [jnp.concatenate(part[:3], axis=1) for part in backward_parts], axis=0
    )
    grad_joined = contract_rows(normed, grad_projected)
    grad_normed = contract_cols(grad_projected, joined)
    attention_pull = jax.vjp(rms_norm, flat_inputs, full_gain.astype(jnp.float32))[1]
    grad_inputs_part, grad_attention_gain = attention_pull(grad_normed)
    input_grad = (grad_middle + grad_inputs_part).reshape(pairs_here, seq_len, model_width)
    grad_relative = sum(part[3] for part in backward_parts)
    grad_table = lax.dot_general(
        rel_hits(tile).astype(jnp.float32),
        grad_relative,
        (((1,), (1,)), ((), ())),
        precision=highest,
    )
    return block_output, input_grad, (
        grad_joined[:, :model_width],
        grad_joined[:, model_width : 2 * model_width],
        grad_joined[:, 2 * model_width :],
        grad_output,
        grad_attention_gain,
        grad_table,
        grad_inner,
        grad_outer,
        grad_ffn_gain,
    )


def gather_all(query_weight, key_weight, value_weight, output_weight, attention_gain, bias_table,
               inner_weight, outer_weight, feedforward_gain):
    return tuple(
        lax.all_gather(part, "fsdp", axis=0, tiled=True)
        for part in (
            query_weight, key_weight, value_weight, output_weight, attention_gain, bias_table,
            inner_weight, outer_weight, feedforward_gain,
        )
    )


def sum_all(gradients):
    def one(part):
        part = lax.psum_scatter(
            part.astype(jnp.bfloat16), "fsdp", scatter_dimension=0, tiled=True
        )
        return lax.psum(part, "rep").astype(jnp.float32)

    return tuple(one(part) for part in gradients)


def gelu_parts(z):
    square = z * z
    t = jnp.tanh(gelu_coeff * z * (1.0 + 0.044715 * square))
    half = 0.5 * (1.0 + t)
    slope = half + (0.5 * gelu_coeff) * z * (1.0 - t * t) * (1.0 + (3 * 0.044715) * square)
    return z * half, slope


def lanes(start, size):
    return pl.ds(start if isinstance(start, int) else pl.multiple_of(start, 128), size)


def rows_at(start, size):
    return pl.ds(pl.multiple_of(start, size), size)


def loop(count, body):
    def step(n, carry):
        body(n)
        return carry

    lax.fori_loop(0, count, step, 0)


def norm_back(grad, gain, values):
    inverse = lax.rsqrt(jnp.mean(values * values, axis=-1, keepdims=True) + epsilon)
    scaled = grad * gain
    centre = jnp.mean(scaled * values, axis=-1, keepdims=True)
    back = inverse * scaled - values * (inverse * inverse * inverse * centre)
    return back, jnp.sum(grad * values * inverse, axis=0, keepdims=True)


class Layer:
    def __init__(self, **refs):
        self.__dict__.update(refs)
        self.seq, self.width = self.x.shape
        self.tile = 128
        self.row_block = 128
        self.shard_rows = self.bank.shape[3]

    def unit(self, u, column=None, size=None):
        if column is None:
            block = self.bank[:, :, u]
        else:
            block = self.bank[:, :, u, :, lanes(column, size)]
        return block.reshape(-1, block.shape[-1])

    def row_chunks(self, body):
        size = self.row_block
        loop(self.seq // size, lambda n: body(rows_at(n * size, size)))

    def small_arrays(self):
        flat = self.all_small[...].reshape(-1, 128)
        tile = self.tile
        slot = lax.broadcasted_iota(jnp.int32, (flat.shape[0], 4 * tile), 1)
        offset = jnp.where(slot < 3 * tile, slot - tile, slot - 5 * tile)
        row = lax.broadcasted_iota(jnp.int32, (flat.shape[0], 4 * tile), 0)
        per = NB // 8
        inside = row % 16 - 2
        wanted = jnp.where((inside >= 0) & (inside < per), (row // 16) * per + inside, -1)
        hits = (bucket_of(offset) == wanted).astype(jnp.bfloat16)
        self.rel[...] = dot_c(flat, hits)[: self.rel.shape[0]]
        for index, ref in ((0, self.gain_a), (1, self.gain_f)):
            total = jnp.zeros((1, self.width), jnp.float32)
            for shard in range(8):
                part = self.all_small[shard].astype(jnp.float32)[index : index + 1]
                wide = jnp.concatenate(
                    [part, jnp.zeros((1, self.width - 128), jnp.float32)], axis=1
                )
                total = total + (
                    pltpu.roll(wide, shard * self.shard_rows, axis=1) if shard else wide
                )
            ref[...] = total

    def norm_in(self):
        gain = self.gain_a[...]

        def body(r):
            self.normed[r] = rms_norm(self.x[r].astype(jnp.float32), gain).astype(jnp.bfloat16)

        self.row_chunks(body)

    def mask_seed(self):
        def body(r):
            index = lax.broadcasted_iota(jnp.int32, (self.row_block, 1), 0) + r.start
            live = index < self.length[0]
            self.seed[r] = jnp.where(live, self.seed[r], jnp.bfloat16(0))

        self.row_chunks(body)

    def project(self, u):
        def body(n):
            self.qkv[u, :, lanes(n * 256, 256)] = dot(
                self.normed[...], self.unit(u, n * 256, 256)
            ).astype(jnp.bfloat16)

        loop(self.width // 256, body)

    def strip_for(self, head, strip):
        tile = self.tile
        rel = self.rel[pl.ds(head, 1), :]
        rolled = pltpu.roll(
            jnp.broadcast_to(rel, (tile, 4 * tile)), 0, axis=1, stride=1, stride_axis=0
        )
        strip[:, 2 * tile : 5 * tile] = rolled[:, : 3 * tile]
        strip[:, : 2 * tile] = jnp.broadcast_to(rel[:, :1], (tile, 2 * tile))
        strip[:, 5 * tile :] = jnp.broadcast_to(rel[:, 3 * tile - 1 : 3 * tile], (tile, 2 * tile))

    def pair_lanes(self, slot):
        third = self.width // 3
        return [lanes(slot * 128 + n * third, 128) for n in range(3)]

    def probs_store(self, pair, slot):
        return pltpu.make_async_copy(
            self.probs.at[slot], self.probs_far.at[pair], self.probs_sems.at[slot]
        )

    def probs_load(self, pair, slot):
        return pltpu.make_async_copy(
            self.probs_far.at[pair], self.probs.at[slot], self.probs_sems.at[slot]
        )

    def attend(self, unit, slot):
        tile, seq = self.tile, self.seq
        pair = 2 * unit + slot
        if unit > 0:
            self.probs_store(pair, slot).wait()
        lane = lax.broadcasted_iota(jnp.int32, (1, 128), 1)
        own = (lane < 64, lane >= 64)
        key_at = lax.broadcasted_iota(jnp.int32, (1, seq), 1)
        mask = jnp.where(key_at < self.length[0], 0.0, masked_score)
        q_at, k_at, v_at = self.pair_lanes(slot)
        q = self.qkv[unit, :, q_at]
        k = self.qkv[unit, :, k_at]
        v = self.qkv[unit, :, v_at]
        for head in range(2):
            self.strip_for(pair * 2 + head, self.strip.at[head])
            self.scores[head] = dot_t(jnp.where(own[head], q, jnp.bfloat16(0)), k)

        def soften(head):
            for block in range(seq // tile):
                r = slice(block * tile, (block + 1) * tile)
                first = (seq // tile - 1 - block) * tile
                bias = self.strip[head, :, first : first + seq]
                scores = self.scores[head, r, :] + (bias + mask)
                peak = jnp.max(scores, axis=-1, keepdims=True)
                raised = jnp.exp(scores - peak)
                total = jnp.sum(raised, axis=-1, keepdims=True)
                self.probs[slot, head, r, :] = (raised * (1.0 / total)).astype(jnp.bfloat16)
            return dot(self.probs[slot, head], v)

        outs = [soften(head) for head in range(2)]
        self.attended[:, lanes(pair * 128, 128)] = jnp.where(own[0], *outs).astype(jnp.bfloat16)
        self.probs_store(pair, slot).start()

    def middle_rows(self):
        def body(n):
            c = lanes(n * 256, 256)
            self.middle[:, c] = self.x[:, c].astype(jnp.float32) + dot(
                self.attended[...], self.unit(3, n * 256, 256)
            )

        loop(self.width // 256, body)
        gain = self.gain_f[...]

        def norm(r):
            self.normed_ffn[r] = rms_norm(self.middle[r], gain).astype(jnp.bfloat16)

        self.row_chunks(norm)

    def raise_unit(self, i):
        def body(n):
            raised = dot(self.normed_ffn[...], self.unit(4 + i, n * 256, 256))
            active, slope = gelu_parts(raised)
            c = lanes(i * self.width + n * 256, 256)
            self.active[:, c] = active.astype(jnp.bfloat16)
            self.slope[:, c] = slope.astype(jnp.bfloat16)

        loop(self.width // 256, body)

    def outer_grad(self, shard):
        size = 4 * self.shard_rows
        block = dot_c(self.active[:, lanes(shard * size, size)], self.seed[...])
        self.bank[shard // 2, shard % 2, 12:16] = block.astype(jnp.bfloat16).reshape(
            4, self.shard_rows, self.width
        )

    def lower(self, n):
        outer = self.bank[:, :, 8:12, :, lanes(n * 256, 256)].reshape(-1, 256)
        c = lanes(n * 256, 256)
        self.mid_low[:, c] = (self.middle[:, c] + dot(self.active[...], outer)).astype(
            jnp.bfloat16
        )

    def raised_grad(self, shard):
        size = 4 * self.shard_rows
        outer = self.bank[shard // 2, shard % 2, 8:12].reshape(size, self.width)
        c = lanes(shard * size, size)
        grad = dot_t(self.seed[...], outer) * self.slope[:, c].astype(jnp.float32)
        self.slope[:, c] = grad.astype(jnp.bfloat16)

    def inner_grad(self, i):
        def body(n):
            c = lanes(i * self.width + n * 256, 256)
            block = dot_c(self.normed_ffn[...], self.slope[:, c]).astype(jnp.bfloat16)
            self.bank[:, :, 16 + i, :, lanes(n * 256, 256)] = block.reshape(
                4, 2, self.shard_rows, 256
            )

        loop(self.width // 256, body)

    def middle_grad(self, part):
        total = None
        for i in range(4):
            inner = self.bank[2 * part : 2 * part + 2, :, 4 + i].reshape(-1, self.width)
            term = dot_t(self.slope[:, i * self.width : (i + 1) * self.width], inner)
            total = term if total is None else total + term
        size = self.width // 2
        self.grad_mid[:, part * size : (part + 1) * size] = total

    def middle_norm(self):
        gain = self.gain_f[...]
        self.gain_f_grad[...] = jnp.zeros_like(self.gain_f_grad)

        def body(r):
            back, terms = norm_back(self.grad_mid[r], gain, self.middle[r])
            total = self.seed[r].astype(jnp.float32) + back
            self.gain_f_grad[...] += terms
            self.grad_mid[r] = total
            self.mid_low[r] = total.astype(jnp.bfloat16)

        self.row_chunks(body)

    def square_grad(self, left, right, slot):
        def body(n):
            block = dot_c(left[...], right(lanes(n * 256, 256))).astype(jnp.bfloat16)
            self.bank[:, :, slot, :, lanes(n * 256, 256)] = block.reshape(
                4, 2, self.shard_rows, 256
            )

        loop(self.width // 256, body)

    def attended_grad(self):
        size = self.width // 2
        for part in range(2):
            weight = self.bank[2 * part : 2 * part + 2, :, 3].reshape(size, self.width)
            self.attended[:, part * size : (part + 1) * size] = dot_t(
                self.mid_low[...], weight
            ).astype(jnp.bfloat16)

    def attend_back(self, unit, slot):
        tile, seq = self.tile, self.seq
        pair = 2 * unit + slot
        self.probs_load(pair, slot).wait()
        lane = lax.broadcasted_iota(jnp.int32, (1, 128), 1)
        own = (lane < 64, lane >= 64)
        q_at, k_at, v_at = self.pair_lanes(slot)
        q = self.qkv[unit, :, q_at]
        k = self.qkv[unit, :, k_at]
        v = self.qkv[unit, :, v_at]
        grad_out = self.attended[:, lanes(pair * 128, 128)]
        blocks = seq // tile
        for head in range(2):
            self.scores[head] = dot_t(jnp.where(own[head], grad_out, jnp.bfloat16(0)), v)

        def back(head):
            sums = [None] * 5
            for block in range(blocks):
                r = slice(block * tile, (block + 1) * tile)
                probs = self.probs[slot, head, r, :].astype(jnp.float32)
                weighted = probs * self.scores[head, r, :]
                centre = jnp.sum(weighted, axis=-1, keepdims=True)
                grad = weighted - probs * centre
                self.grad_scores[head, r, :] = grad.astype(jnp.bfloat16)
                for other in range(blocks):
                    apart = min(2, max(-2, other - block)) + 2
                    part = grad[:, other * tile : (other + 1) * tile]
                    sums[apart] = part if sums[apart] is None else sums[apart] + part
            zero = jnp.zeros((tile, tile), jnp.float32)
            near = shear_sum(jnp.concatenate([sums[1], sums[2], sums[3], zero], axis=1), 4 * tile)
            far = jnp.concatenate(
                [
                    jnp.zeros((1, 2 * tile), jnp.float32),
                    jnp.sum(sums[4], axis=0, keepdims=True),
                    jnp.sum(sums[0], axis=0, keepdims=True),
                ],
                axis=1,
            )
            self.rel_grad[pl.ds(pair * 2 + head, 1), :] = near + far
            return (
                dot(self.grad_scores[head], k),
                dot_c(q, self.grad_scores[head]).T,
                dot_c(grad_out, self.probs[slot, head]).T,
            )

        for at, first, second in zip((q_at, k_at, v_at), back(0), back(1)):
            self.qkv[unit, :, at] = jnp.where(own[0], first, second).astype(jnp.bfloat16)
        if 2 * unit + 2 < self.probs_far.shape[0]:
            self.probs_load(pair + 2, slot).start()

    def normed_grad(self, part):
        size = self.width // 2
        total = None
        for u in range(3):
            weight = self.bank[2 * part : 2 * part + 2, :, u].reshape(size, self.width)
            term = dot_t(self.qkv[u], weight)
            total = term if total is None else total + term
        self.middle[:, part * size : (part + 1) * size] = total

    def input_grad(self):
        gain = self.gain_a[...]
        self.gain_a_grad[...] = jnp.zeros_like(self.gain_a_grad)

        def body(r):
            back, terms = norm_back(self.middle[r], gain, self.x[r].astype(jnp.float32))
            self.gain_a_grad[...] += terms
            self.grad_mid[r] += back

        self.row_chunks(body)

    def small_grads(self):
        tile = self.tile
        shape = (64, 4 * tile)
        slot = lax.broadcasted_iota(jnp.int32, shape, 1)
        offset = jnp.where(slot < 3 * tile, slot - tile, slot - 5 * tile)
        row = lax.broadcasted_iota(jnp.int32, shape, 0)
        per = NB // 8
        inside = row % 8 - 2
        wanted = jnp.where((inside >= 0) & (inside < per), (row // 8) * per + inside, -1)
        hits = (bucket_of(offset) == wanted).astype(jnp.float32)
        table = lax.dot_general(
            hits,
            self.rel_grad[...],
            (((1,), (1,)), ((), ())),
            precision=highest,
            preferred_element_type=jnp.float32,
        )
        rows = lax.broadcasted_iota(jnp.int32, (8, 128), 0)
        lane = lax.broadcasted_iota(jnp.int32, (8, 128), 1)
        for shard in range(8):
            block = table[8 * shard : 8 * shard + 8]
            for index, ref in ((0, self.gain_a_grad), (1, self.gain_f_grad)):
                wide = ref[...]
                if shard:
                    wide = pltpu.roll(wide, self.width - shard * self.shard_rows, axis=1)
                here = (rows == index) & (lane < self.shard_rows)
                block = jnp.where(here, jnp.broadcast_to(wide[:, :128], (8, 128)), block)
            self.small_out[shard] = block


(
    SEND_Z, SEND_X, GOT_SECOND, GOT_BESIDE, GOT_ACROSS, GOT_X, GOT_Y, GOT_CORE, DRAIN, SMALL_Z,
    SMALL_X, SMALL_SECOND, SMALL_BESIDE, SMALL_ACROSS, SUM_SEND, SUM_CORE, SUM_Y, SUM_X, SUM_Z,
    SUM_BACK, SUM_DONE, NORM, PROJECT, ATTEND, MIDDLE, RAISE, OUTER_GRAD, LOWER, RAISED_GRAD,
    INNER_GRAD, MIDDLE_GRAD, MIDDLE_NORM, OUTPUT_GRAD, ATTENDED_GRAD, ATTEND_BACK, SQUARE_GRAD,
    NORMED_GRAD, INPUT_GRAD, SMALL, SMALL_SUM, SMALL_DONE,
) = range(41)

ORDER = (
    (SMALL_Z, 0), (SMALL_X, 0), (SEND_X, 4), (SEND_Z, 1), (SEND_X, 7), (SEND_X, 1), (SEND_X, 2),
    (SEND_X, 0), (SEND_Z, 0), (GOT_SECOND, 1), (GOT_SECOND, 0), (SMALL_SECOND, 0),
    (SMALL_BESIDE, 0), (SMALL_ACROSS, 0), (SEND_X, 6), (SEND_Z, 2), (GOT_BESIDE, 1), (NORM, 0),
    (GOT_ACROSS, 1), (SEND_Z, 3), (GOT_ACROSS, 0), (GOT_BESIDE, 0), (GOT_BESIDE, 2),
    (GOT_SECOND, 2), (GOT_X, 1), (SEND_Z, 5), (GOT_X, 0), (SEND_X, 3), (GOT_ACROSS, 2),
    (GOT_SECOND, 3), (SEND_Z, 4), (GOT_SECOND, 5), (GOT_ACROSS, 3), (GOT_BESIDE, 5), (GOT_Y, 1),
    (GOT_Y, 0), (GOT_X, 2), (GOT_BESIDE, 3), (SEND_Z, 6), (SEND_Z, 11), (SEND_X, 5),
    (GOT_CORE, 1), (PROJECT, 1), (GOT_CORE, 0), (GOT_SECOND, 4), (PROJECT, 0), (SEND_Z, 7),
    (GOT_ACROSS, 5), (GOT_Y, 2), (SEND_X, 11), (GOT_X, 3), (GOT_BESIDE, 4), (ATTEND, 0),
    (GOT_SECOND, 6), (SEND_Z, 9), (GOT_ACROSS, 4), (GOT_X, 5), (GOT_BESIDE, 6), (GOT_CORE, 2),
    (PROJECT, 2), (GOT_BESIDE, 11), (GOT_SECOND, 11), (ATTEND, 1), (GOT_ACROSS, 6), (GOT_X, 4),
    (GOT_Y, 3), (GOT_SECOND, 7), (SEND_Z, 10), (ATTEND, 2), (GOT_Y, 5), (SEND_Z, 8),
    (GOT_ACROSS, 7), (GOT_BESIDE, 7), (GOT_SECOND, 9), (GOT_CORE, 3), (GOT_X, 6), (SEND_X, 9),
    (GOT_Y, 4), (MIDDLE, 0), (GOT_BESIDE, 9), (GOT_ACROSS, 11), (GOT_CORE, 5), (GOT_CORE, 4),
    (RAISE, 0), (GOT_ACROSS, 9), (GOT_X, 7), (GOT_SECOND, 8), (GOT_Y, 6), (RAISE, 1),
    (GOT_ACROSS, 8), (GOT_BESIDE, 8), (GOT_BESIDE, 10), (SEND_X, 8), (GOT_CORE, 6), (RAISE, 2),
    (GOT_X, 11), (GOT_Y, 7), (GOT_SECOND, 10), (OUTER_GRAD, 0), (GOT_X, 9), (GOT_CORE, 7),
    (GOT_ACROSS, 10), (RAISE, 3), (SEND_X, 10), (GOT_X, 8), (GOT_Y, 11), (OUTER_GRAD, 1),
    (GOT_X, 10), (SUM_SEND, 0), (SUM_SEND, 1), (GOT_Y, 9), (SUM_CORE, 0), (GOT_Y, 8),
    (SUM_CORE, 1), (DRAIN, 0), (GOT_Y, 10), (GOT_CORE, 9), (GOT_CORE, 11), (SUM_SEND, 2),
    (GOT_CORE, 8), (SUM_SEND, 3), (GOT_CORE, 10), (RAISED_GRAD, 0), (SUM_Y, 0), (SUM_CORE, 2),
    (INNER_GRAD, 0), (SUM_CORE, 3), (SUM_SEND, 4), (LOWER, 0), (SUM_Y, 1), (RAISED_GRAD, 1),
    (SUM_SEND, 5), (SUM_CORE, 4), (LOWER, 1), (SUM_X, 0), (SUM_Y, 2), (MIDDLE_GRAD, 0),
    (SUM_X, 1), (INNER_GRAD, 1), (SUM_SEND, 6), (SUM_CORE, 5), (SUM_Y, 3), (MIDDLE_GRAD, 1),
    (SUM_CORE, 6), (LOWER, 2), (SUM_X, 2), (SUM_SEND, 7), (MIDDLE_NORM, 0), (SUM_Y, 4),
    (OUTPUT_GRAD, 0), (ATTENDED_GRAD, 0), (SUM_X, 3), (SUM_SEND, 8), (SUM_CORE, 7),
    (ATTEND_BACK, 0), (SUM_X, 4), (SUM_Y, 5), (SUM_CORE, 8), (ATTEND_BACK, 1), (SUM_Y, 7),
    (SUM_Z, 4), (SUM_X, 5), (SQUARE_GRAD, 0), (SUM_SEND, 9), (SQUARE_GRAD, 1), (SUM_Y, 8),
    (SUM_Z, 0), (SUM_SEND, 10), (SUM_Y, 6), (SUM_Z, 1), (SUM_CORE, 9), (SUM_X, 7),
    (ATTEND_BACK, 2), (SUM_X, 8), (SUM_CORE, 10), (SQUARE_GRAD, 2), (SUM_Y, 9), (SUM_SEND, 11),
    (SUM_X, 6), (SUM_CORE, 11), (SUM_Z, 3), (SUM_Z, 2), (SUM_BACK, 4), (NORMED_GRAD, 0),
    (SUM_Y, 10), (NORMED_GRAD, 1), (SUM_X, 9), (INPUT_GRAD, 0), (SUM_BACK, 1), (SUM_Y, 11),
    (SUM_Z, 5), (SUM_Z, 7), (SUM_Z, 8), (SUM_X, 10), (SUM_BACK, 2), (SUM_BACK, 5), (SUM_DONE, 2),
    (SUM_Z, 6), (SUM_X, 11), (SUM_BACK, 6), (SMALL, 0), (SUM_BACK, 7), (SUM_BACK, 3), (SUM_Z, 10),
    (SUM_Z, 9), (SMALL_SUM, 0), (SUM_BACK, 0), (SUM_Z, 11), (SUM_DONE, 5), (SUM_DONE, 3),
    (SUM_DONE, 1), (SUM_BACK, 10), (SUM_BACK, 8), (SUM_DONE, 0), (SMALL_DONE, 0), (SUM_DONE, 8),
    (SUM_DONE, 6), (SUM_BACK, 9), (SUM_BACK, 11), (SUM_DONE, 9), (SUM_DONE, 10), (SUM_DONE, 7),
    (SUM_DONE, 4), (SUM_DONE, 11),
)


def order_slot(n):
    return n + 12 if n < 8 else (7 if n == 8 else n - 5)


def fused_kernel(
    length, x, cot, gain_a_own, gain_f_own, table_own, query_own, key_own, value_own, output_own,
    inner_own, outer_own,
    block_far, grad_far, own_far, small_result, probs_far,
    bank, own_sum, from_core, from_y, from_x, from_z, small_wide, all_small, small_out,
    small_in, small_rep, probs, normed, qkv, attended, middle, normed_ffn, active, slope, seed,
    grad_mid, mid_low, scores, rel, rel_grad, gain_a, gain_f, gain_a_grad,
    gain_f_grad, strip, grad_scores,
    sends, recvs, sum_sends, sum_recvs, small_sends, small_recvs, back_sems, probs_sems,
    misc_sems, keep_sems,
):
    shard = lax.axis_index("fsdp")
    copy_id = lax.axis_index("rep")
    layer = Layer(
        length=length, x=x, bank=bank, all_small=all_small, small_out=small_out,
        probs=probs, probs_far=probs_far, probs_sems=probs_sems, normed=normed, qkv=qkv,
        attended=attended, middle=middle, normed_ffn=normed_ffn, active=active, slope=slope,
        seed=seed, grad_mid=grad_mid, mid_low=mid_low, scores=scores,
        rel=rel, rel_grad=rel_grad, gain_a=gain_a, gain_f=gain_f, gain_a_grad=gain_a_grad,
        gain_f_grad=gain_f_grad, strip=strip, grad_scores=grad_scores,
    )
    rows, width = query_own.shape
    chunks = inner_own.shape[1] // width
    units = 4 + 2 * chunks
    gather = Gather(bank, sends, recvs)
    scatter = Scatter(
        order_slot, bank, own_sum, from_core, from_y, from_x, from_z, sum_sends, sum_recvs
    )
    pairs = probs_far.shape[0]

    def remote(src, dst, send, recv, device):
        return pltpu.make_async_remote_copy(
            src_ref=src, dst_ref=dst, send_sem=send, recv_sem=recv, device_id=device,
            device_id_type=MESH,
        )

    def peer(k):
        return (lax.rem(shard + k, 8), copy_id)

    def rep_peer(k):
        return (shard, lax.rem(copy_id + k, 4))

    parts = [output_own]
    parts += [inner_own.at[:, pl.ds(i * width, width)] for i in range(chunks)]
    parts += [outer_own.at[pl.ds(i * rows, rows)] for i in range(chunks)]
    third = width // 3
    homes = [
        (part.at[:, pl.ds(u * third, third)], bank.at[gather.z, gather.x, u, :, pl.ds(n * third, third)])
        for u in range(3)
        for n, part in enumerate((query_own, key_own, value_own))
    ]
    homes += [(part, bank.at[gather.z, gather.x, 3 + u]) for u, part in enumerate(parts)]
    keeps = [
        pltpu.make_async_copy(part, home, keep_sems.at[0]) for part, home in homes
    ]
    keep_seed = pltpu.make_async_copy(cot, seed, keep_sems.at[1])
    keeps.append(keep_seed)
    peers = gather.peers()
    greet(peers, gather.at_end)
    for copy in keeps:
        copy.start()
    small_wide[...] = jnp.zeros_like(small_wide)
    small_wide[0:1, :rows] = gain_a_own[...].astype(jnp.float32)
    small_wide[1:2, :rows] = gain_f_own[...].astype(jnp.float32)
    per, heads = table_own.shape
    small_wide[2 : 2 + per, :heads] = table_own[...].astype(jnp.float32)
    all_small[shard] = small_wide[...].astype(jnp.bfloat16)
    smalls = SmallGather(gather, all_small, small_sends, small_recvs)
    mine = bank.at[gather.z, gather.x, 0:units]
    pltpu.make_async_copy(mine, mine, keep_sems.at[0]).wait()
    all_greeted(peers, gather.at_end)

    def store(n):
        return pltpu.make_async_copy(own_sum.at[n], own_far.at[n], misc_sems.at[2])

    def sum_done(n):
        scatter.after_back_core(n)
        store(n).start()

    block_store = pltpu.make_async_copy(mid_low, block_far, misc_sems.at[0])
    grad_store = pltpu.make_async_copy(grad_mid, grad_far, misc_sems.at[1])
    back_copies = [
        remote(
            small_out.at[lax.rem(shard + k, 8)], small_in.at[k - 1], back_sems.at[0],
            back_sems.at[1], peer(k),
        )
        for k in range(1, 8)
    ]
    rep_copies = [
        remote(
            small_rep.at[copy_id], small_rep.at[copy_id], back_sems.at[2], back_sems.at[3],
            rep_peer(k),
        )
        for k in range(1, 4)
    ]

    def wait_for(part, sem):
        pltpu.make_async_copy(part, part, sem).wait()

    def norm(_):
        keep_seed.wait()
        layer.mask_seed()
        smalls.after_x(0)
        layer.small_arrays()
        layer.norm_in()

    def middle_rows(_):
        layer.middle_rows()
        for pair in (pairs - 2, pairs - 1):
            layer.probs_store(pair, pair % 2).wait()
        for pair in (0, 1):
            layer.probs_load(pair, pair).start()

    def lower(n):
        layer.lower(n)
        if n == width // 256 - 1:
            block_store.start()

    def middle_norm(_):
        block_store.wait()
        layer.middle_norm()
        rel_grad[...] = jnp.zeros_like(rel_grad)

    def input_grad(_):
        layer.input_grad()
        grad_store.start()

    def small_sums(_):
        layer.small_grads()
        for copy in back_copies:
            copy.start()

    def small_sum(_):
        wait_for(small_in, back_sems.at[1])
        total = small_out[shard]
        for k in range(7):
            total = total + small_in[k]
        small_rep[copy_id] = total
        for copy in rep_copies:
            copy.start()

    def small_done(_):
        wait_for(small_rep.at[0:3], back_sems.at[3])
        small_result[...] = (small_rep[0] + small_rep[1]) + (small_rep[2] + small_rep[3])

    work = {
        SEND_Z: gather.send_z,
        SEND_X: gather.send_x,
        GOT_SECOND: gather.after_second,
        GOT_BESIDE: gather.after_beside,
        GOT_ACROSS: gather.after_across,
        GOT_X: gather.after_x,
        GOT_Y: gather.after_y,
        GOT_CORE: gather.after_core,
        DRAIN: gather.drain,
        SMALL_Z: smalls.send_z,
        SMALL_X: smalls.send_x,
        SMALL_SECOND: smalls.after_second,
        SMALL_BESIDE: smalls.after_beside,
        SMALL_ACROSS: smalls.after_across,
        SUM_SEND: scatter.start,
        SUM_CORE: scatter.after_core,
        SUM_Y: scatter.after_y,
        SUM_X: scatter.after_x,
        SUM_Z: scatter.after_z,
        SUM_BACK: scatter.after_back_y,
        SUM_DONE: sum_done,
        NORM: norm,
        PROJECT: layer.project,
        ATTEND: lambda u: loop(2, functools.partial(layer.attend, u)),
        MIDDLE: middle_rows,
        RAISE: layer.raise_unit,
        OUTER_GRAD: lambda k: loop(4, lambda n: layer.outer_grad(4 * k + n)),
        LOWER: lower,
        RAISED_GRAD: lambda k: loop(4, lambda n: layer.raised_grad(4 * k + n)),
        INNER_GRAD: lambda k: loop(2, lambda n: layer.inner_grad(2 * k + n)),
        MIDDLE_GRAD: layer.middle_grad,
        MIDDLE_NORM: middle_norm,
        OUTPUT_GRAD: lambda _: layer.square_grad(attended, lambda c: mid_low[:, c], 7),
        ATTENDED_GRAD: lambda _: layer.attended_grad(),
        ATTEND_BACK: lambda u: loop(2, functools.partial(layer.attend_back, u)),
        SQUARE_GRAD: lambda u: layer.square_grad(normed, lambda c: qkv[u, :, c], 4 + u),
        NORMED_GRAD: layer.normed_grad,
        INPUT_GRAD: input_grad,
        SMALL: small_sums,
        SMALL_SUM: small_sum,
        SMALL_DONE: small_done,
    }
    for name, n in ORDER:
        work[name](n)
    gather.drain(1)
    smalls.drain(0)
    scatter.drain()
    wait_for(small_in, back_sems.at[0])
    wait_for(small_rep.at[0:3], back_sems.at[2])
    wait_for(own_sum, misc_sems.at[2])
    grad_store.wait()


def fused_call(length, x, cot, gain_a, gain_f, table, square, inner, outer):
    rows, width = square[0].shape
    units = 4 + 2 * (inner.shape[1] // width)
    heads = table.shape[1]
    seq = x.shape[0]
    half = rows // 2
    part = half // 3
    hidden = inner.shape[1]
    low, wide = jnp.bfloat16, jnp.float32
    anywhere = pl.BlockSpec(memory_space=pl.ANY)
    within = pl.BlockSpec(memory_space=pltpu.VMEM)
    sems = pltpu.SemaphoreType.DMA
    vm = pltpu.VMEM
    head_rows = -(-heads // 8) * 8
    return pl.pallas_call(
        fused_kernel,
        out_shape=(
            jax.ShapeDtypeStruct((seq, width), low),
            jax.ShapeDtypeStruct((seq, width), wide),
            jax.ShapeDtypeStruct((units, rows, width), low),
            jax.ShapeDtypeStruct((8, 128), wide),
            jax.ShapeDtypeStruct((heads // 2, 2, seq, seq), low),
        ),
        in_specs=[pl.BlockSpec(memory_space=pltpu.SMEM), within, anywhere]
        + [within] * 3
        + [anywhere] * 6,
        out_specs=[anywhere, anywhere, anywhere, within, anywhere],
        scratch_shapes=[
            vm((4, 2, units + 8, rows, width), low),
            vm((units, rows, width), low),
            vm((6, 4, 2, half, width), low),
            vm((units, 4, 2, part, width), low),
            vm((units, 4, 2 * part, width), low),
            vm((units, 4, 2 * part, width), low),
            vm((16, 128), wide),
            vm((8, 16, 128), low),
            vm((8, 8, 128), wide),
            vm((7, 8, 128), wide),
            vm((4, 8, 128), wide),
            vm((2, 2, seq, seq), low),
            vm((seq, width), low),
            vm((3, seq, width), low),
            vm((seq, width), low),
            vm((seq, width), wide),
            vm((seq, width), low),
            vm((seq, hidden), low),
            vm((seq, hidden), low),
            vm((seq, width), low),
            vm((seq, width), wide),
            vm((seq, width), low),
            vm((2, seq, seq), wide),
            vm((head_rows, 512), wide),
            vm((128, 512), wide),
            vm((1, width), wide),
            vm((1, width), wide),
            vm((1, width), wide),
            vm((1, width), wide),
            vm((2, 128, 128 * 7), wide),
            vm((2, seq, seq), low),
            sems((2,)),
            sems((units, Gather.slots)),
            sems((4 + units,)),
            sems((units, Scatter.slots)),
            sems((1,)),
            sems((4,)),
            sems((4,)),
            sems((2,)),
            sems((3,)),
            sems((2,)),
        ],
        compiler_params=pltpu.CompilerParams(
            collective_id=0, has_side_effects=True, vmem_limit_bytes=63 * 2**20
        ),
    )(length, x, cot, gain_a, gain_f, table, *square, inner, outer)


def finish_kernel(
    block_in, grad_in, sums_far, small, block_out, grad_out, query_out, key_out, value_out,
    output_out, gain_a, table, inner_out, outer_out, gain_f, block, grad, query, key, value, output,
    inner, outer, sums, in_sems, out_sems,
):
    units, rows, width = sums.shape
    chunks = inner.shape[1] // width
    third = width // 3
    straight = ((block_in, block, block_out), (grad_in, grad, grad_out))
    loads = [pltpu.make_async_copy(sums_far.at[n], sums.at[n], in_sems.at[n]) for n in range(units)]
    loads += [
        pltpu.make_async_copy(far, near, in_sems.at[units + n])
        for n, (far, near, _) in enumerate(straight)
    ]
    for copy in loads[units:] + loads[:units]:
        copy.start()
    stores = []

    def store(near, far):
        stores.append(pltpu.make_async_copy(near, far, out_sems.at[len(stores)]))
        stores[-1].start()

    for n, (_, near, far) in enumerate(straight):
        loads[units + n].wait()
        store(near, far)
    gain_a[...] = small[0:1, :rows]
    gain_f[...] = small[1:2, :rows]
    table[...] = small[2 : 2 + table.shape[0], : table.shape[1]]
    for i in range(chunks):
        part = pl.ds(i * rows, rows)
        loads[i].wait()
        outer[part, :] = sums[i].astype(jnp.float32)
        store(outer.at[part], outer_out.at[part])
    for i in range(chunks):
        part = pl.ds(i * width, width)
        loads[chunks + i].wait()
        inner[:, part] = sums[chunks + i].astype(jnp.float32)
        store(inner.at[:, part], inner_out.at[:, part])
    loads[2 * chunks].wait()
    output[...] = sums[2 * chunks].astype(jnp.float32)
    store(output, output_out)
    for u in range(3):
        loads[2 * chunks + 1 + u].wait()
        for n, ref in enumerate((query, key, value)):
            ref[:, u * third : (u + 1) * third] = sums[
                2 * chunks + 1 + u, :, n * third : (n + 1) * third
            ].astype(jnp.float32)
    for near, far in ((query, query_out), (key, key_out), (value, value_out)):
        store(near, far)
    for copy in stores:
        copy.wait()


def finish_call(block, grad, sums, small, table_shape, inner_shape, outer_shape):
    units, rows, width = sums.shape
    wide = jnp.float32
    anywhere = pl.BlockSpec(memory_space=pl.ANY)
    within = pl.BlockSpec(memory_space=pltpu.VMEM)
    shapes = [(rows, width)] * 4 + [(1, rows), table_shape, inner_shape, outer_shape, (1, rows)]
    places = [anywhere] * 4 + [within] * 2 + [anywhere] * 2 + [within]
    staged = [shape for shape, place in zip(shapes, places) if place is anywhere]
    return pl.pallas_call(
        finish_kernel,
        out_shape=[
            jax.ShapeDtypeStruct(block.shape, block.dtype),
            jax.ShapeDtypeStruct(grad.shape, grad.dtype),
        ]
        + [jax.ShapeDtypeStruct(shape, wide) for shape in shapes],
        in_specs=[anywhere, anywhere, anywhere, within],
        out_specs=[anywhere, anywhere] + places,
        scratch_shapes=[
            pltpu.VMEM(block.shape, block.dtype),
            pltpu.VMEM(grad.shape, grad.dtype),
            *[pltpu.VMEM(shape, wide) for shape in staged],
            pltpu.VMEM(sums.shape, sums.dtype),
            pltpu.SemaphoreType.DMA((units + 2,)),
            pltpu.SemaphoreType.DMA((units + 2,)),
        ],
        compiler_params=pltpu.CompilerParams(vmem_limit_bytes=63 * 2**20),
    )(block, grad, sums, small)


def local_linked(
    inputs, lengths, cotangent, query_weight, key_weight, value_weight, output_weight,
    attention_gain, bias_table, inner_weight, outer_weight, feedforward_gain,
):
    rows = query_weight.shape[0]
    square = (query_weight, key_weight, value_weight, output_weight)
    block, grad, sums, small, _ = fused_call(
        lengths, inputs[0], cotangent[0], attention_gain.reshape(1, rows),
        feedforward_gain.reshape(1, rows), bias_table, square, inner_weight, outer_weight,
    )
    block, grad, query, key, value, output, gain_a, table, inner, outer, gain_f = finish_call(
        block, grad, sums, small, bias_table.shape, inner_weight.shape, outer_weight.shape
    )
    return (
        block[None], grad[None], query, key, value, output, gain_a.reshape(rows), table, inner,
        outer, gain_f.reshape(rows),
    )


def local(inputs, lengths, cotangent, *shards):
    block_output, input_grad, gradients = compute(inputs, lengths, cotangent, gather_all(*shards))
    return (block_output, input_grad) + sum_all(gradients)


def can_link(mesh):
    return mesh.shape["fsdp"] == 8 and mesh.shape["rep"] == 4


def solution(mesh):
    placed = (
        P(("fsdp", "rep"), None, None),
        P(("fsdp", "rep")),
        P(("fsdp", "rep"), None, None),
        P("fsdp", None),
        P("fsdp", None),
        P("fsdp", None),
        P("fsdp", None),
        P("fsdp"),
        P("fsdp", None),
        P("fsdp", None),
        P("fsdp", None),
        P("fsdp"),
    )
    return jax.shard_map(
        local_linked if can_link(mesh) else local,
        mesh=mesh,
        in_specs=placed,
        out_specs=(
            P(("fsdp", "rep"), None, None),
            P(("fsdp", "rep"), None, None),
            P("fsdp", None),
            P("fsdp", None),
            P("fsdp", None),
            P("fsdp", None),
            P("fsdp"),
            P("fsdp", None),
            P("fsdp", None),
            P("fsdp", None),
            P("fsdp"),
        ),
        check_vma=False,
    )
```

profile of v0, /device:TPU:1, one launch (start us, length us, event | category | flops | bytes accessed | tf_op | source)
XLA Modules:
  0.0 148.6 jit_solution(13674983677653185802)
XLA Ops:
  1.3 141.7 %shard_map.203 = (bf16[512,768]{1,0:T(8,128)(2,1)}, f32[512,768]{1,0:T(8,128)}, bf16[12,96,768]{2,1,0:T(8,128)(2,1)}, f32[8,128]{1,0:T(8,128)}, bf16[6,2,512,512]{3,2,1,0:T(8,128)(2,1)}) custom-call(s32[1]{0:T(128)S(6)} %copy.23.length, bf16[512,768]{1,0:T(8,128)(2,1)} %bitcast.8, bf16[512,768]{1,0:T(8,128)(2,1)} %bitcast.9, bf16[1,96]{1,0:T(2,128)(2,1)} %bitcast.10, ...), custom_call_target="tpu_custom_call" | custom-call | tf_op jit(solution)/shard_map/pallas_call | solution.py:1188
  143.0 5.4 %shard_map.204 = (bf16[512,768]{1,0:T(8,128)(2,1)}, f32[512,768]{1,0:T(8,128)}, f32[96,768]{1,0:T(8,128)}, f32[96,768]{1,0:T(8,128)}, f32[96,768]{1,0:T(8,128)},...) custom-call(bf16[512,768]{1,0:T(8,128)(2,1)} %get-tuple-element.26.b, ...), custom_call_target="tpu_custom_call" | custom-call | tf_op jit(solution)/shard_map/pallas_call | solution.py:1311
where the time goes:
time: 149 us
  Pallas kernels  147 us (99%)
    pallas_call x1, Pallas kernels, fused_call(): pl.pallas_call(fused_kernel, out_shape=(jax.ShapeDtypeStruct((seq, width)...  142 us
    pallas_call x1, Pallas kernels, finish_call(): pl.pallas_call(finish_kernel, out_shape=[jax.ShapeDtypeStruct(block.shape...  5.42 us

commit v1 on v0

--- a/solution.py
+++ b/solution.py
@@ -928,43 +928,43 @@
 
 ORDER = (
     (SMALL_Z, 0), (SMALL_X, 0), (SEND_X, 4), (SEND_Z, 1), (SEND_X, 7), (SEND_X, 1), (SEND_X, 2),
-    (SEND_X, 0), (SEND_Z, 0), (GOT_SECOND, 1), (GOT_SECOND, 0), (SMALL_SECOND, 0),
-    (SMALL_BESIDE, 0), (SMALL_ACROSS, 0), (SEND_X, 6), (SEND_Z, 2), (GOT_BESIDE, 1), (NORM, 0),
-    (GOT_ACROSS, 1), (SEND_Z, 3), (GOT_ACROSS, 0), (GOT_BESIDE, 0), (GOT_BESIDE, 2),
-    (GOT_SECOND, 2), (GOT_X, 1), (SEND_Z, 5), (GOT_X, 0), (SEND_X, 3), (GOT_ACROSS, 2),
-    (GOT_SECOND, 3), (SEND_Z, 4), (GOT_SECOND, 5), (GOT_ACROSS, 3), (GOT_BESIDE, 5), (GOT_Y, 1),
-    (GOT_Y, 0), (GOT_X, 2), (GOT_BESIDE, 3), (SEND_Z, 6), (SEND_Z, 11), (SEND_X, 5),
-    (GOT_CORE, 1), (PROJECT, 1), (GOT_CORE, 0), (GOT_SECOND, 4), (PROJECT, 0), (SEND_Z, 7),
-    (GOT_ACROSS, 5), (GOT_Y, 2), (SEND_X, 11), (GOT_X, 3), (GOT_BESIDE, 4), (ATTEND, 0),
-    (GOT_SECOND, 6), (SEND_Z, 9), (GOT_ACROSS, 4), (GOT_X, 5), (GOT_BESIDE, 6), (GOT_CORE, 2),
-    (PROJECT, 2), (GOT_BESIDE, 11), (GOT_SECOND, 11), (ATTEND, 1), (GOT_ACROSS, 6), (GOT_X, 4),
-    (GOT_Y, 3), (GOT_SECOND, 7), (SEND_Z, 10), (ATTEND, 2), (GOT_Y, 5), (SEND_Z, 8),
-    (GOT_ACROSS, 7), (GOT_BESIDE, 7), (GOT_SECOND, 9), (GOT_CORE, 3), (GOT_X, 6), (SEND_X, 9),
-    (GOT_Y, 4), (MIDDLE, 0), (GOT_BESIDE, 9), (GOT_ACROSS, 11), (GOT_CORE, 5), (GOT_CORE, 4),
-    (RAISE, 0), (GOT_ACROSS, 9), (GOT_X, 7), (GOT_SECOND, 8), (GOT_Y, 6), (RAISE, 1),
-    (GOT_ACROSS, 8), (GOT_BESIDE, 8), (GOT_BESIDE, 10), (SEND_X, 8), (GOT_CORE, 6), (RAISE, 2),
-    (GOT_X, 11), (GOT_Y, 7), (GOT_SECOND, 10), (OUTER_GRAD, 0), (GOT_X, 9), (GOT_CORE, 7),
-    (GOT_ACROSS, 10), (RAISE, 3), (SEND_X, 10), (GOT_X, 8), (GOT_Y, 11), (OUTER_GRAD, 1),
-    (GOT_X, 10), (SUM_SEND, 0), (SUM_SEND, 1), (GOT_Y, 9), (SUM_CORE, 0), (GOT_Y, 8),
-    (SUM_CORE, 1), (DRAIN, 0), (GOT_Y, 10), (GOT_CORE, 9), (GOT_CORE, 11), (SUM_SEND, 2),
-    (GOT_CORE, 8), (SUM_SEND, 3), (GOT_CORE, 10), (RAISED_GRAD, 0), (SUM_Y, 0), (SUM_CORE, 2),
-    (INNER_GRAD, 0), (SUM_CORE, 3), (SUM_SEND, 4), (LOWER, 0), (SUM_Y, 1), (RAISED_GRAD, 1),
-    (SUM_SEND, 5), (SUM_CORE, 4), (LOWER, 1), (SUM_X, 0), (SUM_Y, 2), (MIDDLE_GRAD, 0),
-    (SUM_X, 1), (INNER_GRAD, 1), (SUM_SEND, 6), (SUM_CORE, 5), (SUM_Y, 3), (MIDDLE_GRAD, 1),
-    (SUM_CORE, 6), (LOWER, 2), (SUM_X, 2), (SUM_SEND, 7), (MIDDLE_NORM, 0), (SUM_Y, 4),
-    (OUTPUT_GRAD, 0), (ATTENDED_GRAD, 0), (SUM_X, 3), (SUM_SEND, 8), (SUM_CORE, 7),
-    (ATTEND_BACK, 0), (SUM_X, 4), (SUM_Y, 5), (SUM_CORE, 8), (ATTEND_BACK, 1), (SUM_Y, 7),
-    (SUM_Z, 4), (SUM_X, 5), (SQUARE_GRAD, 0), (SUM_SEND, 9), (SQUARE_GRAD, 1), (SUM_Y, 8),
-    (SUM_Z, 0), (SUM_SEND, 10), (SUM_Y, 6), (SUM_Z, 1), (SUM_CORE, 9), (SUM_X, 7),
-    (ATTEND_BACK, 2), (SUM_X, 8), (SUM_CORE, 10), (SQUARE_GRAD, 2), (SUM_Y, 9), (SUM_SEND, 11),
-    (SUM_X, 6), (SUM_CORE, 11), (SUM_Z, 3), (SUM_Z, 2), (SUM_BACK, 4), (NORMED_GRAD, 0),
-    (SUM_Y, 10), (NORMED_GRAD, 1), (SUM_X, 9), (INPUT_GRAD, 0), (SUM_BACK, 1), (SUM_Y, 11),
-    (SUM_Z, 5), (SUM_Z, 7), (SUM_Z, 8), (SUM_X, 10), (SUM_BACK, 2), (SUM_BACK, 5), (SUM_DONE, 2),
-    (SUM_Z, 6), (SUM_X, 11), (SUM_BACK, 6), (SMALL, 0), (SUM_BACK, 7), (SUM_BACK, 3), (SUM_Z, 10),
-    (SUM_Z, 9), (SMALL_SUM, 0), (SUM_BACK, 0), (SUM_Z, 11), (SUM_DONE, 5), (SUM_DONE, 3),
-    (SUM_DONE, 1), (SUM_BACK, 10), (SUM_BACK, 8), (SUM_DONE, 0), (SMALL_DONE, 0), (SUM_DONE, 8),
-    (SUM_DONE, 6), (SUM_BACK, 9), (SUM_BACK, 11), (SUM_DONE, 9), (SUM_DONE, 10), (SUM_DONE, 7),
-    (SUM_DONE, 4), (SUM_DONE, 11),
+    (SEND_X, 0), (SEND_Z, 0), (GOT_SECOND, 1), (GOT_SECOND, 0), (SEND_X, 6), (SEND_Z, 2),
+    (GOT_BESIDE, 1), (SMALL_SECOND, 0), (SMALL_BESIDE, 0), (GOT_ACROSS, 1), (SMALL_ACROSS, 0),
+    (SEND_Z, 3), (GOT_ACROSS, 0), (GOT_BESIDE, 0), (GOT_BESIDE, 2), (GOT_SECOND, 2), (GOT_X, 1),
+    (SEND_Z, 5), (GOT_X, 0), (SEND_X, 3), (GOT_ACROSS, 2), (GOT_SECOND, 3), (SEND_Z, 4),
+    (GOT_SECOND, 5), (GOT_ACROSS, 3), (GOT_BESIDE, 5), (NORM, 0), (GOT_Y, 1), (GOT_Y, 0),
+    (GOT_X, 2), (GOT_BESIDE, 3), (SEND_Z, 6), (SEND_Z, 11), (SEND_X, 5), (GOT_CORE, 1),
+    (PROJECT, 1), (GOT_CORE, 0), (GOT_SECOND, 4), (PROJECT, 0), (SEND_Z, 7), (GOT_ACROSS, 5),
+    (GOT_Y, 2), (SEND_X, 11), (GOT_X, 3), (GOT_BESIDE, 4), (ATTEND, 0), (GOT_SECOND, 6),
+    (SEND_Z, 9), (GOT_ACROSS, 4), (GOT_X, 5), (GOT_BESIDE, 6), (GOT_CORE, 2), (PROJECT, 2),
+    (GOT_BESIDE, 11), (GOT_SECOND, 11), (ATTEND, 1), (GOT_ACROSS, 6), (GOT_X, 4), (GOT_Y, 3),
+    (GOT_SECOND, 7), (SEND_Z, 10), (ATTEND, 2), (GOT_Y, 5), (SEND_Z, 8), (GOT_ACROSS, 7),
+    (GOT_BESIDE, 7), (GOT_SECOND, 9), (GOT_CORE, 3), (GOT_X, 6), (SEND_X, 9), (GOT_Y, 4),
+    (MIDDLE, 0), (GOT_BESIDE, 9), (GOT_ACROSS, 11), (GOT_CORE, 5), (GOT_CORE, 4), (RAISE, 0),
+    (GOT_ACROSS, 9), (GOT_X, 7), (GOT_SECOND, 8), (GOT_Y, 6), (RAISE, 1), (GOT_ACROSS, 8),
+    (GOT_BESIDE, 8), (GOT_BESIDE, 10), (SEND_X, 8), (GOT_CORE, 6), (RAISE, 2), (GOT_X, 11),
+    (GOT_Y, 7), (GOT_SECOND, 10), (OUTER_GRAD, 0), (GOT_X, 9), (GOT_CORE, 7), (GOT_ACROSS, 10),
+    (RAISE, 3), (SEND_X, 10), (GOT_X, 8), (GOT_Y, 11), (OUTER_GRAD, 1), (GOT_X, 10),
+    (SUM_SEND, 0), (SUM_SEND, 1), (GOT_Y, 9), (SUM_CORE, 0), (GOT_Y, 8), (SUM_CORE, 1),
+    (DRAIN, 0), (GOT_Y, 10), (GOT_CORE, 9), (GOT_CORE, 11), (SUM_SEND, 2), (GOT_CORE, 8),
+    (SUM_SEND, 3), (GOT_CORE, 10), (RAISED_GRAD, 0), (SUM_Y, 0), (SUM_CORE, 2), (INNER_GRAD, 0),
+    (SUM_CORE, 3), (SUM_SEND, 4), (LOWER, 0), (SUM_Y, 1), (RAISED_GRAD, 1), (SUM_SEND, 5),
+    (SUM_CORE, 4), (LOWER, 1), (SUM_X, 0), (SUM_Y, 2), (MIDDLE_GRAD, 0), (SUM_X, 1),
+    (INNER_GRAD, 1), (SUM_SEND, 6), (SUM_CORE, 5), (SUM_Y, 3), (MIDDLE_GRAD, 1), (SUM_CORE, 6),
+    (LOWER, 2), (SUM_X, 2), (SUM_SEND, 7), (MIDDLE_NORM, 0), (SUM_Y, 4), (OUTPUT_GRAD, 0),
+    (ATTENDED_GRAD, 0), (SUM_X, 3), (SUM_SEND, 8), (SUM_CORE, 7), (ATTEND_BACK, 0), (SUM_X, 4),
+    (SUM_Y, 5), (SUM_CORE, 8), (ATTEND_BACK, 1), (SUM_Y, 7), (SUM_Z, 4), (SUM_X, 5),
+    (SQUARE_GRAD, 0), (SUM_SEND, 9), (SQUARE_GRAD, 1), (SUM_Y, 8), (SUM_Z, 0), (SUM_SEND, 10),
+    (SUM_Y, 6), (SUM_Z, 1), (SUM_CORE, 9), (SUM_X, 7), (ATTEND_BACK, 2), (SUM_X, 8),
+    (SUM_CORE, 10), (SQUARE_GRAD, 2), (SUM_Y, 9), (SUM_SEND, 11), (SUM_X, 6), (SUM_CORE, 11),
+    (SUM_Z, 3), (SUM_Z, 2), (SUM_BACK, 4), (NORMED_GRAD, 0), (SUM_Y, 10), (NORMED_GRAD, 1),
+    (SUM_X, 9), (INPUT_GRAD, 0), (SUM_BACK, 1), (SUM_Y, 11), (SUM_Z, 5), (SUM_Z, 7), (SUM_Z, 8),
+    (SUM_X, 10), (SUM_BACK, 2), (SUM_BACK, 5), (SUM_DONE, 2), (SUM_Z, 6), (SUM_X, 11),
+    (SUM_BACK, 6), (SMALL, 0), (SUM_BACK, 7), (SUM_BACK, 3), (SUM_Z, 10), (SUM_Z, 9),
+    (SMALL_SUM, 0), (SUM_BACK, 0), (SUM_Z, 11), (SUM_DONE, 5), (SUM_DONE, 3), (SUM_DONE, 1),
+    (SUM_BACK, 10), (SUM_BACK, 8), (SUM_DONE, 0), (SMALL_DONE, 0), (SUM_DONE, 8), (SUM_DONE, 6),
+    (SUM_BACK, 9), (SUM_BACK, 11), (SUM_DONE, 9), (SUM_DONE, 10), (SUM_DONE, 7), (SUM_DONE, 4),
+    (SUM_DONE, 11),
 )
 
 

time: 149 us -> 148 us (level)
  no operation moved by 1% of the time
where the time goes in v1:
time: 148 us; the launch traced here: 147 us
  Pallas kernels  146 us (99%)
  between operations  1.48 us (1%)
    pallas_call x1, Pallas kernels, fused_call(): pl.pallas_call(fused_kernel, out_shape=(jax.ShapeDtypeStruct((seq, width)...  141 us
    pallas_call x1, Pallas kernels, finish_call(): pl.pallas_call(finish_kernel, out_shape=[jax.ShapeDtypeStruct(block.shape...  5.42 us

profile of v1, /device:TPU:1, one launch (start us, length us, event | category | flops | bytes accessed | tf_op | source)
XLA Modules:
  0.0 147.5 jit_solution(1723306536320306169)
XLA Ops:
  1.3 140.6 %shard_map.203 = (bf16[512,768]{1,0:T(8,128)(2,1)}, f32[512,768]{1,0:T(8,128)}, bf16[12,96,768]{2,1,0:T(8,128)(2,1)}, f32[8,128]{1,0:T(8,128)}, bf16[6,2,512,512]{3,2,1,0:T(8,128)(2,1)}) custom-call(s32[1]{0:T(128)S(6)} %copy.23.length, bf16[512,768]{1,0:T(8,128)(2,1)} %bitcast.8, bf16[512,768]{1,0:T(8,128)(2,1)} %bitcast.9, bf16[1,96]{1,0:T(2,128)(2,1)} %bitcast.10, ...), custom_call_target="tpu_custom_call" | custom-call | tf_op jit(solution)/shard_map/pallas_call | solution.py:1188
  141.9 5.4 %shard_map.204 = (bf16[512,768]{1,0:T(8,128)(2,1)}, f32[512,768]{1,0:T(8,128)}, f32[96,768]{1,0:T(8,128)}, f32[96,768]{1,0:T(8,128)}, f32[96,768]{1,0:T(8,128)},...) custom-call(bf16[512,768]{1,0:T(8,128)(2,1)} %get-tuple-element.26.b, ...), custom_call_target="tpu_custom_call" | custom-call | tf_op jit(solution)/shard_map/pallas_call | solution.py:1311

commit v2 on v1

--- a/solution.py
+++ b/solution.py
@@ -232,7 +232,7 @@
 
 
 class Gather(Links):
-    slots = 6
+    slots = 7
 
     def __init__(self, full, send_sems, recv_sems):
         super().__init__(full.shape[3], send_sems, recv_sems)
@@ -290,14 +290,21 @@
         pl.when(~self.at_end)(lambda: self.z_copy(g, self.across, 2).start())
 
     def send_x(self, g):
-        self.x_copy(g, self.z).start()
+        part = self.block(g, self.z, self.plane)
+        self.move(part, g, 6 if g % 3 == 2 else 3, self.to_x()).start()
+
+    def pass_beside(self, g):
+        part = self.full.at[self.z, 1 - self.x, g, self.plane]
+        self.arrived(part, g, 6)
+        self.move(part, g, 3, self.at_z(self.beside)).start()
 
     def spread(self, g, a, slot):
         self.arrived(self.block(g, a, self.plane), g, slot)
         if slot == 0:
             part = self.block(g, a, self.plane)
             pl.when(~self.at_end)(lambda: self.move(part, g, 2, self.at_z(self.beside)).start())
-        self.x_copy(g, a).start()
+        if slot != 1 or g % 3 != 2:
+            self.x_copy(g, a).start()
         self.y_copy(g, a).start()
 
     def after_second(self, g):
@@ -310,7 +317,9 @@
         self.spread(g, self.across, 2)
 
     def after_x(self, g):
-        self.arrived(self.column(g, self.plane), g, 3)
+        rows = self.plane.size
+        part = self.full.at[0, 0, 0:3, 0:rows] if g % 3 == 2 else self.column(g, self.plane)
+        self.arrived(part, g, 3)
         self.move(self.column(g, self.own_third), g, 4, self.to_y()).start()
 
     def after_y(self, g):
@@ -377,6 +386,16 @@
 
 class Scatter(Links):
     slots = 6
+    whole = (0, 2)
+
+    def rows(self, g):
+        return self.half if g in self.whole else self.plane
+
+    def count(self, g):
+        return self.rows(g).size
+
+    def sender(self, g, n):
+        return 3 + n + self.own.shape[0] if g in self.whole else n
 
     def __init__(self, slot, full, own, from_core, from_y, from_x, from_z, send_sems, recv_sems):
         super().__init__(own.shape[1], send_sems, recv_sems)
@@ -393,16 +412,18 @@
         return self.copy(part, self.from_y.at[g], g, 1, 1, self.to_y())
 
     def x_copy(self, g):
-        part = self.full.at[:, 1 - self.x, self.slot(g), self.plane]
-        return self.copy(part, self.from_x.at[g], g, 1, 2, self.to_x())
+        part = self.full.at[:, 1 - self.x, self.slot(g), self.rows(g)]
+        there = self.from_x.at[g, :, 0 : self.count(g)]
+        return self.copy(part, there, g, self.sender(g, 1), 2, self.to_x())
 
     def z_copy(self, g, k):
-        part = self.full.at[lax.rem(self.z + k, 4), self.x, self.slot(g), self.plane]
-        return self.copy(part, self.from_z.at[g, k - 1], g, 2, 3, self.to_z(k))
+        part = self.full.at[lax.rem(self.z + k, 4), self.x, self.slot(g), self.rows(g)]
+        there = self.from_z.at[g, k - 1, 0 : self.count(g)]
+        return self.copy(part, there, g, self.sender(g, 2), 3, self.to_z(k))
 
     def back_y_copy(self, g):
-        part = self.own.at[g, self.plane]
-        return self.copy(part, self.from_z.at[g, 3], g, 4 + g, 4, self.to_y())
+        part = self.own.at[g, self.rows(g)]
+        return self.copy(part, self.from_z.at[g, 3, 0 : self.count(g)], g, 4 + g, 4, self.to_y())
 
     def back_core_copy(self, g):
         part = self.own.at[g, self.half]
@@ -417,7 +438,7 @@
         for a in range(4):
             for b in range(2):
                 self.full[a, b, self.slot(g), self.half] += self.from_core[ring, a, b]
-        self.y_copy(g).start()
+        (self.x_copy(g) if g in self.whole else self.y_copy(g)).start()
 
     def after_y(self, g):
         self.y_copy(g).wait_recv()
@@ -429,25 +450,29 @@
     def after_x(self, g):
         self.x_copy(g).wait_recv()
         for a in range(4):
-            self.full[a, self.x, self.slot(g), self.plane] += self.from_x[g, a]
+            part = self.from_x[g, a, 0 : self.count(g)]
+            self.full[a, self.x, self.slot(g), self.rows(g)] += part
         for k in (1, 2, 3):
             self.z_copy(g, k).start()
 
     def after_z(self, g):
-        total = self.full[self.z, self.x, self.slot(g), self.plane].astype(jnp.float32)
-        part = self.from_z.at[g, 0:3]
+        total = self.full[self.z, self.x, self.slot(g), self.rows(g)].astype(jnp.float32)
+        part = self.from_z.at[g, 0:3, 0 : self.count(g)]
         pltpu.make_async_copy(part, part, self.recv_sems.at[g, 3]).wait()
         for k in (1, 2, 3):
-            total = total + self.from_z[g, k - 1].astype(jnp.float32)
-        self.own[g, self.plane] = total.astype(jnp.bfloat16)
+            total = total + self.from_z[g, k - 1, 0 : self.count(g)].astype(jnp.float32)
+        self.own[g, self.rows(g)] = total.astype(jnp.bfloat16)
         self.back_y_copy(g).start()
 
     def after_back_y(self, g):
         self.back_y_copy(g).wait_recv()
         self.back_y_copy(g).wait_send()
         got = self.from_z.at[g, 3]
-        self.own[g, self.shared] += got[self.shared_in]
-        self.own[g, self.other_third] = got[self.third_in]
+        if g in self.whole:
+            self.own[g, self.half] += got[...]
+        else:
+            self.own[g, self.shared] += got[self.shared_in]
+            self.own[g, self.other_third] = got[self.third_in]
         self.back_core_copy(g).start()
 
     def after_back_core(self, g):
@@ -456,12 +481,15 @@
 
     def drain(self):
         units, rows = self.own.shape[:2]
-        half = rows // 2
+        few = len(self.whole)
+        part = rows // 3
         for n, part in (
             (0, self.full.at[:, :, 0 : units // 2]),
-            (1, self.full.at[:, :, 0 : units // 3]),
-            (2, self.full.at[:, :, 0 : units // 4, 0:half]),
+            (1, self.full.at[:, :, 0 : units - few, 0:part]),
+            (2, self.from_z.at[0 : units - few, 0:3, 0:part]),
             (3, self.own.at[0 : units // 2]),
+            (4 + units, self.from_x.at[0:few]),
+            (5 + units, self.from_z.at[0:few, 0:3]),
         ):
             pltpu.make_async_copy(part, part, self.send_sems.at[n]).wait()
 
@@ -919,52 +947,52 @@
 
 
 (
-    SEND_Z, SEND_X, GOT_SECOND, GOT_BESIDE, GOT_ACROSS, GOT_X, GOT_Y, GOT_CORE, DRAIN, SMALL_Z,
-    SMALL_X, SMALL_SECOND, SMALL_BESIDE, SMALL_ACROSS, SUM_SEND, SUM_CORE, SUM_Y, SUM_X, SUM_Z,
-    SUM_BACK, SUM_DONE, NORM, PROJECT, ATTEND, MIDDLE, RAISE, OUTER_GRAD, LOWER, RAISED_GRAD,
-    INNER_GRAD, MIDDLE_GRAD, MIDDLE_NORM, OUTPUT_GRAD, ATTENDED_GRAD, ATTEND_BACK, SQUARE_GRAD,
-    NORMED_GRAD, INPUT_GRAD, SMALL, SMALL_SUM, SMALL_DONE,
-) = range(41)
+    SEND_Z, SEND_X, GOT_SECOND, GOT_BESIDE, GOT_ACROSS, GOT_X, GOT_Y, GOT_CORE, DRAIN,
+    PASS_BESIDE, SMALL_Z, SMALL_X, SMALL_SECOND, SMALL_BESIDE, SMALL_ACROSS, SUM_SEND, SUM_CORE,
+    SUM_Y, SUM_X, SUM_Z, SUM_BACK, SUM_DONE, NORM, PROJECT, ATTEND, MIDDLE, RAISE, OUTER_GRAD,
+    LOWER, RAISED_GRAD, INNER_GRAD, MIDDLE_GRAD, MIDDLE_NORM, OUTPUT_GRAD, ATTENDED_GRAD,
+    ATTEND_BACK, SQUARE_GRAD, NORMED_GRAD, INPUT_GRAD, SMALL, SMALL_SUM, SMALL_DONE,
+) = range(42)
 
 ORDER = (
-    (SMALL_Z, 0), (SMALL_X, 0), (SEND_X, 4), (SEND_Z, 1), (SEND_X, 7), (SEND_X, 1), (SEND_X, 2),
-    (SEND_X, 0), (SEND_Z, 0), (GOT_SECOND, 1), (GOT_SECOND, 0), (SEND_X, 6), (SEND_Z, 2),
-    (GOT_BESIDE, 1), (SMALL_SECOND, 0), (SMALL_BESIDE, 0), (GOT_ACROSS, 1), (SMALL_ACROSS, 0),
-    (SEND_Z, 3), (GOT_ACROSS, 0), (GOT_BESIDE, 0), (GOT_BESIDE, 2), (GOT_SECOND, 2), (GOT_X, 1),
-    (SEND_Z, 5), (GOT_X, 0), (SEND_X, 3), (GOT_ACROSS, 2), (GOT_SECOND, 3), (SEND_Z, 4),
-    (GOT_SECOND, 5), (GOT_ACROSS, 3), (GOT_BESIDE, 5), (NORM, 0), (GOT_Y, 1), (GOT_Y, 0),
-    (GOT_X, 2), (GOT_BESIDE, 3), (SEND_Z, 6), (SEND_Z, 11), (SEND_X, 5), (GOT_CORE, 1),
-    (PROJECT, 1), (GOT_CORE, 0), (GOT_SECOND, 4), (PROJECT, 0), (SEND_Z, 7), (GOT_ACROSS, 5),
-    (GOT_Y, 2), (SEND_X, 11), (GOT_X, 3), (GOT_BESIDE, 4), (ATTEND, 0), (GOT_SECOND, 6),
-    (SEND_Z, 9), (GOT_ACROSS, 4), (GOT_X, 5), (GOT_BESIDE, 6), (GOT_CORE, 2), (PROJECT, 2),
-    (GOT_BESIDE, 11), (GOT_SECOND, 11), (ATTEND, 1), (GOT_ACROSS, 6), (GOT_X, 4), (GOT_Y, 3),
-    (GOT_SECOND, 7), (SEND_Z, 10), (ATTEND, 2), (GOT_Y, 5), (SEND_Z, 8), (GOT_ACROSS, 7),
-    (GOT_BESIDE, 7), (GOT_SECOND, 9), (GOT_CORE, 3), (GOT_X, 6), (SEND_X, 9), (GOT_Y, 4),
-    (MIDDLE, 0), (GOT_BESIDE, 9), (GOT_ACROSS, 11), (GOT_CORE, 5), (GOT_CORE, 4), (RAISE, 0),
-    (GOT_ACROSS, 9), (GOT_X, 7), (GOT_SECOND, 8), (GOT_Y, 6), (RAISE, 1), (GOT_ACROSS, 8),
-    (GOT_BESIDE, 8), (GOT_BESIDE, 10), (SEND_X, 8), (GOT_CORE, 6), (RAISE, 2), (GOT_X, 11),
-    (GOT_Y, 7), (GOT_SECOND, 10), (OUTER_GRAD, 0), (GOT_X, 9), (GOT_CORE, 7), (GOT_ACROSS, 10),
-    (RAISE, 3), (SEND_X, 10), (GOT_X, 8), (GOT_Y, 11), (OUTER_GRAD, 1), (GOT_X, 10),
-    (SUM_SEND, 0), (SUM_SEND, 1), (GOT_Y, 9), (SUM_CORE, 0), (GOT_Y, 8), (SUM_CORE, 1),
-    (DRAIN, 0), (GOT_Y, 10), (GOT_CORE, 9), (GOT_CORE, 11), (SUM_SEND, 2), (GOT_CORE, 8),
-    (SUM_SEND, 3), (GOT_CORE, 10), (RAISED_GRAD, 0), (SUM_Y, 0), (SUM_CORE, 2), (INNER_GRAD, 0),
-    (SUM_CORE, 3), (SUM_SEND, 4), (LOWER, 0), (SUM_Y, 1), (RAISED_GRAD, 1), (SUM_SEND, 5),
-    (SUM_CORE, 4), (LOWER, 1), (SUM_X, 0), (SUM_Y, 2), (MIDDLE_GRAD, 0), (SUM_X, 1),
-    (INNER_GRAD, 1), (SUM_SEND, 6), (SUM_CORE, 5), (SUM_Y, 3), (MIDDLE_GRAD, 1), (SUM_CORE, 6),
-    (LOWER, 2), (SUM_X, 2), (SUM_SEND, 7), (MIDDLE_NORM, 0), (SUM_Y, 4), (OUTPUT_GRAD, 0),
-    (ATTENDED_GRAD, 0), (SUM_X, 3), (SUM_SEND, 8), (SUM_CORE, 7), (ATTEND_BACK, 0), (SUM_X, 4),
-    (SUM_Y, 5), (SUM_CORE, 8), (ATTEND_BACK, 1), (SUM_Y, 7), (SUM_Z, 4), (SUM_X, 5),
-    (SQUARE_GRAD, 0), (SUM_SEND, 9), (SQUARE_GRAD, 1), (SUM_Y, 8), (SUM_Z, 0), (SUM_SEND, 10),
-    (SUM_Y, 6), (SUM_Z, 1), (SUM_CORE, 9), (SUM_X, 7), (ATTEND_BACK, 2), (SUM_X, 8),
-    (SUM_CORE, 10), (SQUARE_GRAD, 2), (SUM_Y, 9), (SUM_SEND, 11), (SUM_X, 6), (SUM_CORE, 11),
-    (SUM_Z, 3), (SUM_Z, 2), (SUM_BACK, 4), (NORMED_GRAD, 0), (SUM_Y, 10), (NORMED_GRAD, 1),
-    (SUM_X, 9), (INPUT_GRAD, 0), (SUM_BACK, 1), (SUM_Y, 11), (SUM_Z, 5), (SUM_Z, 7), (SUM_Z, 8),
-    (SUM_X, 10), (SUM_BACK, 2), (SUM_BACK, 5), (SUM_DONE, 2), (SUM_Z, 6), (SUM_X, 11),
-    (SUM_BACK, 6), (SMALL, 0), (SUM_BACK, 7), (SUM_BACK, 3), (SUM_Z, 10), (SUM_Z, 9),
-    (SMALL_SUM, 0), (SUM_BACK, 0), (SUM_Z, 11), (SUM_DONE, 5), (SUM_DONE, 3), (SUM_DONE, 1),
-    (SUM_BACK, 10), (SUM_BACK, 8), (SUM_DONE, 0), (SMALL_DONE, 0), (SUM_DONE, 8), (SUM_DONE, 6),
-    (SUM_BACK, 9), (SUM_BACK, 11), (SUM_DONE, 9), (SUM_DONE, 10), (SUM_DONE, 7), (SUM_DONE, 4),
-    (SUM_DONE, 11),
+    (SMALL_Z, 0), (SMALL_X, 0), (SEND_X, 7), (SEND_Z, 0), (SEND_X, 3), (SEND_X, 4), (SEND_X, 2),
+    (GOT_SECOND, 0), (SEND_X, 0), (SEND_X, 9), (SEND_Z, 1), (GOT_ACROSS, 0), (SEND_Z, 2),
+    (SEND_X, 1), (GOT_BESIDE, 0), (SMALL_SECOND, 0), (SMALL_BESIDE, 0), (SMALL_ACROSS, 0),
+    (GOT_SECOND, 1), (GOT_BESIDE, 1), (PASS_BESIDE, 2), (GOT_ACROSS, 1), (SEND_Z, 3),
+    (GOT_BESIDE, 2), (GOT_SECOND, 2), (GOT_X, 0), (SEND_Z, 4), (NORM, 0), (GOT_ACROSS, 2),
+    (GOT_SECOND, 3), (GOT_X, 1), (GOT_BESIDE, 3), (SEND_Z, 7), (GOT_ACROSS, 3), (GOT_BESIDE, 4),
+    (GOT_Y, 0), (GOT_SECOND, 4), (GOT_CORE, 0), (SEND_Z, 6), (GOT_X, 2), (SEND_X, 5), (SEND_Z, 5),
+    (PROJECT, 0), (GOT_ACROSS, 4), (GOT_Y, 1), (GOT_X, 3), (GOT_SECOND, 7), (ATTEND, 0),
+    (GOT_CORE, 1), (GOT_BESIDE, 7), (PROJECT, 1), (SEND_Z, 9), (SEND_X, 6), (GOT_X, 4),
+    (GOT_Y, 2), (GOT_ACROSS, 7), (GOT_SECOND, 6), (GOT_BESIDE, 6), (ATTEND, 1), (GOT_ACROSS, 6),
+    (GOT_Y, 3), (GOT_CORE, 2), (GOT_SECOND, 5), (GOT_X, 7), (SEND_X, 11), (PASS_BESIDE, 5),
+    (GOT_ACROSS, 5), (SEND_Z, 8), (PROJECT, 2), (GOT_SECOND, 9), (GOT_X, 6), (SEND_X, 8),
+    (SEND_Z, 11), (GOT_CORE, 3), (GOT_BESIDE, 5), (ATTEND, 2), (SEND_Z, 10), (GOT_Y, 7),
+    (GOT_X, 5), (GOT_SECOND, 8), (GOT_Y, 4), (MIDDLE, 0), (GOT_Y, 6), (GOT_BESIDE, 9),
+    (GOT_BESIDE, 8), (GOT_ACROSS, 9), (GOT_CORE, 7), (PASS_BESIDE, 11), (RAISE, 3), (GOT_CORE, 4),
+    (GOT_BESIDE, 10), (GOT_CORE, 6), (GOT_SECOND, 11), (GOT_Y, 5), (PASS_BESIDE, 8),
+    (GOT_ACROSS, 8), (GOT_BESIDE, 11), (RAISE, 2), (GOT_ACROSS, 11), (GOT_SECOND, 10), (GOT_X, 9),
+    (GOT_CORE, 5), (DRAIN, 0), (RAISE, 0), (GOT_X, 8), (GOT_ACROSS, 10), (RAISE, 1), (SEND_X, 10),
+    (GOT_X, 11), (OUTER_GRAD, 1), (GOT_X, 10), (GOT_Y, 8), (GOT_Y, 9), (OUTER_GRAD, 0),
+    (GOT_Y, 11), (SUM_SEND, 0), (GOT_Y, 10), (GOT_CORE, 9), (SUM_SEND, 1), (GOT_CORE, 8),
+    (SUM_CORE, 0), (SUM_SEND, 2), (GOT_CORE, 11), (SUM_SEND, 3), (GOT_CORE, 10), (RAISED_GRAD, 0),
+    (SUM_CORE, 1), (INNER_GRAD, 0), (SUM_SEND, 4), (SUM_CORE, 2), (LOWER, 0), (SUM_SEND, 5),
+    (SUM_CORE, 3), (SUM_X, 0), (RAISED_GRAD, 1), (SUM_CORE, 4), (MIDDLE_GRAD, 0), (SUM_Y, 1),
+    (INNER_GRAD, 1), (SUM_SEND, 6), (SUM_X, 2), (LOWER, 1), (SUM_CORE, 5), (SUM_SEND, 7),
+    (LOWER, 2), (SUM_Y, 4), (SUM_Y, 3), (MIDDLE_GRAD, 1), (SUM_CORE, 6), (SUM_X, 1),
+    (MIDDLE_NORM, 0), (OUTPUT_GRAD, 0), (ATTENDED_GRAD, 0), (SUM_CORE, 7), (SUM_X, 4),
+    (ATTEND_BACK, 0), (SUM_SEND, 8), (SUM_Y, 5), (SUM_X, 3), (SUM_Y, 6), (SQUARE_GRAD, 0),
+    (SUM_SEND, 9), (SUM_CORE, 8), (ATTEND_BACK, 1), (SUM_CORE, 9), (SUM_X, 5), (SUM_Y, 7),
+    (ATTEND_BACK, 2), (SUM_X, 6), (SUM_Z, 1), (SUM_Z, 3), (SUM_Y, 9), (SQUARE_GRAD, 1),
+    (SUM_SEND, 10), (SQUARE_GRAD, 2), (SUM_X, 7), (SUM_Y, 8), (SUM_SEND, 11), (SUM_CORE, 10),
+    (SUM_CORE, 11), (SUM_X, 9), (NORMED_GRAD, 0), (SUM_Y, 10), (NORMED_GRAD, 1), (SUM_Z, 6),
+    (SUM_BACK, 3), (SUM_X, 8), (INPUT_GRAD, 0), (SUM_Y, 11), (SUM_Z, 9), (SMALL, 0), (SUM_Z, 0),
+    (SUM_X, 10), (SUM_Z, 8), (SUM_Z, 7), (SUM_BACK, 0), (SUM_Z, 4), (SMALL_SUM, 0), (SUM_Z, 2),
+    (SUM_X, 11), (SUM_BACK, 8), (SUM_Z, 10), (SUM_Z, 5), (SUM_Z, 11), (SUM_BACK, 2),
+    (SUM_BACK, 7), (SUM_DONE, 0), (SUM_BACK, 4), (SMALL_DONE, 0), (SUM_DONE, 3), (SUM_BACK, 10),
+    (SUM_BACK, 5), (SUM_BACK, 1), (SUM_DONE, 7), (SUM_BACK, 6), (SUM_BACK, 9), (SUM_DONE, 5),
+    (SUM_BACK, 11), (SUM_DONE, 2), (SUM_DONE, 1), (SUM_DONE, 6), (SUM_DONE, 9), (SUM_DONE, 8),
+    (SUM_DONE, 4), (SUM_DONE, 10), (SUM_DONE, 11),
 )
 
 
@@ -1127,6 +1155,7 @@
         GOT_Y: gather.after_y,
         GOT_CORE: gather.after_core,
         DRAIN: gather.drain,
+        PASS_BESIDE: gather.pass_beside,
         SMALL_Z: smalls.send_z,
         SMALL_X: smalls.send_x,
         SMALL_SECOND: smalls.after_second,
@@ -1203,8 +1232,8 @@
             vm((units, rows, width), low),
             vm((6, 4, 2, half, width), low),
             vm((units, 4, 2, part, width), low),
-            vm((units, 4, 2 * part, width), low),
-            vm((units, 4, 2 * part, width), low),
+            vm((units, 4, half, width), low),
+            vm((units, 4, half, width), low),
             vm((16, 128), wide),
             vm((8, 16, 128), low),
             vm((8, 8, 128), wide),
@@ -1232,7 +1261,7 @@
             vm((2, seq, seq), low),
             sems((2,)),
             sems((units, Gather.slots)),
-            sems((4 + units,)),
+            sems((6 + units,)),
             sems((units, Scatter.slots)),
             sems((1,)),
             sems((4,)),

time: 148 us -> 143 us (0.966)
  Pallas kernels: 146 us -> 141 us
    pallas_call x1, Pallas kernels: 141 us -> 136 us  [fused_call(): pl.pallas_call(fused_kernel, out_shape=(jax.ShapeDtypeStruct((seq, width)...]
where the time goes in v2:
time: 143 us
  Pallas kernels  141 us (99%)
  between operations  1.48 us (1%)
    pallas_call x1, Pallas kernels, fused_call(): pl.pallas_call(fused_kernel, out_shape=(jax.ShapeDtypeStruct((seq, width)...  136 us
    pallas_call x1, Pallas kernels, finish_call(): pl.pallas_call(finish_kernel, out_shape=[jax.ShapeDtypeStruct(block.shape...  5.42 us

profile of v2, /device:TPU:1, one launch (start us, length us, event | category | flops | bytes accessed | tf_op | source)
XLA Modules:
  0.0 142.8 jit_solution(1748882109404110954)
XLA Ops:
  1.3 135.9 %shard_map.203 = (bf16[512,768]{1,0:T(8,128)(2,1)}, f32[512,768]{1,0:T(8,128)}, bf16[12,96,768]{2,1,0:T(8,128)(2,1)}, f32[8,128]{1,0:T(8,128)}, bf16[6,2,512,512]{3,2,1,0:T(8,128)(2,1)}) custom-call(s32[1]{0:T(128)S(6)} %copy.23.length, bf16[512,768]{1,0:T(8,128)(2,1)} %bitcast.8, bf16[512,768]{1,0:T(8,128)(2,1)} %bitcast.9, bf16[1,96]{1,0:T(2,128)(2,1)} %bitcast.10, ...), custom_call_target="tpu_custom_call" | custom-call | tf_op jit(solution)/shard_map/pallas_call | solution.py:1217
  137.2 5.4 %shard_map.204 = (bf16[512,768]{1,0:T(8,128)(2,1)}, f32[512,768]{1,0:T(8,128)}, f32[96,768]{1,0:T(8,128)}, f32[96,768]{1,0:T(8,128)}, f32[96,768]{1,0:T(8,128)},...) custom-call(bf16[512,768]{1,0:T(8,128)(2,1)} %get-tuple-element.26.b, ...), custom_call_target="tpu_custom_call" | custom-call | tf_op jit(solution)/shard_map/pallas_call | solution.py:1340

commit v3 on v2

--- a/solution.py
+++ b/solution.py
@@ -955,44 +955,44 @@
 ) = range(42)
 
 ORDER = (
-    (SMALL_Z, 0), (SMALL_X, 0), (SEND_X, 7), (SEND_Z, 0), (SEND_X, 3), (SEND_X, 4), (SEND_X, 2),
-    (GOT_SECOND, 0), (SEND_X, 0), (SEND_X, 9), (SEND_Z, 1), (GOT_ACROSS, 0), (SEND_Z, 2),
-    (SEND_X, 1), (GOT_BESIDE, 0), (SMALL_SECOND, 0), (SMALL_BESIDE, 0), (SMALL_ACROSS, 0),
-    (GOT_SECOND, 1), (GOT_BESIDE, 1), (PASS_BESIDE, 2), (GOT_ACROSS, 1), (SEND_Z, 3),
-    (GOT_BESIDE, 2), (GOT_SECOND, 2), (GOT_X, 0), (SEND_Z, 4), (NORM, 0), (GOT_ACROSS, 2),
-    (GOT_SECOND, 3), (GOT_X, 1), (GOT_BESIDE, 3), (SEND_Z, 7), (GOT_ACROSS, 3), (GOT_BESIDE, 4),
-    (GOT_Y, 0), (GOT_SECOND, 4), (GOT_CORE, 0), (SEND_Z, 6), (GOT_X, 2), (SEND_X, 5), (SEND_Z, 5),
-    (PROJECT, 0), (GOT_ACROSS, 4), (GOT_Y, 1), (GOT_X, 3), (GOT_SECOND, 7), (ATTEND, 0),
-    (GOT_CORE, 1), (GOT_BESIDE, 7), (PROJECT, 1), (SEND_Z, 9), (SEND_X, 6), (GOT_X, 4),
-    (GOT_Y, 2), (GOT_ACROSS, 7), (GOT_SECOND, 6), (GOT_BESIDE, 6), (ATTEND, 1), (GOT_ACROSS, 6),
-    (GOT_Y, 3), (GOT_CORE, 2), (GOT_SECOND, 5), (GOT_X, 7), (SEND_X, 11), (PASS_BESIDE, 5),
-    (GOT_ACROSS, 5), (SEND_Z, 8), (PROJECT, 2), (GOT_SECOND, 9), (GOT_X, 6), (SEND_X, 8),
-    (SEND_Z, 11), (GOT_CORE, 3), (GOT_BESIDE, 5), (ATTEND, 2), (SEND_Z, 10), (GOT_Y, 7),
-    (GOT_X, 5), (GOT_SECOND, 8), (GOT_Y, 4), (MIDDLE, 0), (GOT_Y, 6), (GOT_BESIDE, 9),
-    (GOT_BESIDE, 8), (GOT_ACROSS, 9), (GOT_CORE, 7), (PASS_BESIDE, 11), (RAISE, 3), (GOT_CORE, 4),
-    (GOT_BESIDE, 10), (GOT_CORE, 6), (GOT_SECOND, 11), (GOT_Y, 5), (PASS_BESIDE, 8),
-    (GOT_ACROSS, 8), (GOT_BESIDE, 11), (RAISE, 2), (GOT_ACROSS, 11), (GOT_SECOND, 10), (GOT_X, 9),
-    (GOT_CORE, 5), (DRAIN, 0), (RAISE, 0), (GOT_X, 8), (GOT_ACROSS, 10), (RAISE, 1), (SEND_X, 10),
-    (GOT_X, 11), (OUTER_GRAD, 1), (GOT_X, 10), (GOT_Y, 8), (GOT_Y, 9), (OUTER_GRAD, 0),
-    (GOT_Y, 11), (SUM_SEND, 0), (GOT_Y, 10), (GOT_CORE, 9), (SUM_SEND, 1), (GOT_CORE, 8),
-    (SUM_CORE, 0), (SUM_SEND, 2), (GOT_CORE, 11), (SUM_SEND, 3), (GOT_CORE, 10), (RAISED_GRAD, 0),
-    (SUM_CORE, 1), (INNER_GRAD, 0), (SUM_SEND, 4), (SUM_CORE, 2), (LOWER, 0), (SUM_SEND, 5),
-    (SUM_CORE, 3), (SUM_X, 0), (RAISED_GRAD, 1), (SUM_CORE, 4), (MIDDLE_GRAD, 0), (SUM_Y, 1),
-    (INNER_GRAD, 1), (SUM_SEND, 6), (SUM_X, 2), (LOWER, 1), (SUM_CORE, 5), (SUM_SEND, 7),
-    (LOWER, 2), (SUM_Y, 4), (SUM_Y, 3), (MIDDLE_GRAD, 1), (SUM_CORE, 6), (SUM_X, 1),
-    (MIDDLE_NORM, 0), (OUTPUT_GRAD, 0), (ATTENDED_GRAD, 0), (SUM_CORE, 7), (SUM_X, 4),
-    (ATTEND_BACK, 0), (SUM_SEND, 8), (SUM_Y, 5), (SUM_X, 3), (SUM_Y, 6), (SQUARE_GRAD, 0),
-    (SUM_SEND, 9), (SUM_CORE, 8), (ATTEND_BACK, 1), (SUM_CORE, 9), (SUM_X, 5), (SUM_Y, 7),
-    (ATTEND_BACK, 2), (SUM_X, 6), (SUM_Z, 1), (SUM_Z, 3), (SUM_Y, 9), (SQUARE_GRAD, 1),
-    (SUM_SEND, 10), (SQUARE_GRAD, 2), (SUM_X, 7), (SUM_Y, 8), (SUM_SEND, 11), (SUM_CORE, 10),
-    (SUM_CORE, 11), (SUM_X, 9), (NORMED_GRAD, 0), (SUM_Y, 10), (NORMED_GRAD, 1), (SUM_Z, 6),
-    (SUM_BACK, 3), (SUM_X, 8), (INPUT_GRAD, 0), (SUM_Y, 11), (SUM_Z, 9), (SMALL, 0), (SUM_Z, 0),
-    (SUM_X, 10), (SUM_Z, 8), (SUM_Z, 7), (SUM_BACK, 0), (SUM_Z, 4), (SMALL_SUM, 0), (SUM_Z, 2),
-    (SUM_X, 11), (SUM_BACK, 8), (SUM_Z, 10), (SUM_Z, 5), (SUM_Z, 11), (SUM_BACK, 2),
-    (SUM_BACK, 7), (SUM_DONE, 0), (SUM_BACK, 4), (SMALL_DONE, 0), (SUM_DONE, 3), (SUM_BACK, 10),
-    (SUM_BACK, 5), (SUM_BACK, 1), (SUM_DONE, 7), (SUM_BACK, 6), (SUM_BACK, 9), (SUM_DONE, 5),
-    (SUM_BACK, 11), (SUM_DONE, 2), (SUM_DONE, 1), (SUM_DONE, 6), (SUM_DONE, 9), (SUM_DONE, 8),
-    (SUM_DONE, 4), (SUM_DONE, 10), (SUM_DONE, 11),
+    (SMALL_Z, 0), (SMALL_X, 0), (SEND_Z, 0), (SEND_X, 5), (SEND_X, 0), (SEND_X, 3), (SEND_X, 7),
+    (SEND_X, 1), (GOT_BESIDE, 0), (SMALL_SECOND, 0), (SMALL_BESIDE, 0), (SEND_Z, 1), (SEND_Z, 2),
+    (GOT_SECOND, 0), (SEND_X, 2), (GOT_ACROSS, 0), (SMALL_ACROSS, 0), (PASS_BESIDE, 5),
+    (GOT_BESIDE, 1), (GOT_SECOND, 1), (SEND_Z, 4), (PASS_BESIDE, 2), (GOT_BESIDE, 2), (GOT_X, 0),
+    (GOT_ACROSS, 1), (GOT_SECOND, 2), (SEND_Z, 3), (NORM, 0), (SEND_X, 4), (GOT_BESIDE, 4),
+    (GOT_X, 1), (GOT_ACROSS, 2), (SEND_Z, 7), (GOT_SECOND, 3), (GOT_SECOND, 4), (GOT_Y, 0),
+    (GOT_X, 2), (GOT_Y, 1), (GOT_BESIDE, 3), (GOT_CORE, 0), (SEND_Z, 6), (GOT_ACROSS, 3),
+    (GOT_SECOND, 7), (PROJECT, 0), (GOT_BESIDE, 7), (GOT_ACROSS, 4), (SEND_Z, 5), (SEND_X, 6),
+    (GOT_CORE, 1), (GOT_Y, 2), (PROJECT, 1), (GOT_X, 3), (GOT_BESIDE, 6), (GOT_CORE, 2),
+    (GOT_SECOND, 6), (SEND_Z, 9), (ATTEND, 0), (GOT_ACROSS, 7), (GOT_Y, 3), (GOT_X, 4),
+    (GOT_SECOND, 5), (GOT_BESIDE, 5), (SEND_Z, 8), (GOT_ACROSS, 6), (SEND_X, 8), (SEND_Z, 11),
+    (ATTEND, 1), (GOT_X, 7), (GOT_BESIDE, 9), (GOT_ACROSS, 5), (SEND_X, 11), (PROJECT, 2),
+    (GOT_X, 6), (ATTEND, 2), (GOT_SECOND, 9), (GOT_SECOND, 8), (GOT_Y, 7), (SEND_Z, 10),
+    (PASS_BESIDE, 8), (SEND_X, 9), (GOT_BESIDE, 11), (GOT_CORE, 3), (MIDDLE, 0), (GOT_Y, 6),
+    (GOT_CORE, 7), (GOT_X, 5), (GOT_ACROSS, 9), (GOT_Y, 4), (GOT_ACROSS, 8), (RAISE, 3),
+    (GOT_CORE, 6), (SEND_X, 10), (GOT_BESIDE, 8), (GOT_SECOND, 11), (RAISE, 2), (GOT_ACROSS, 11),
+    (PASS_BESIDE, 11), (GOT_X, 8), (GOT_X, 9), (GOT_Y, 5), (GOT_SECOND, 10), (OUTER_GRAD, 1),
+    (GOT_ACROSS, 10), (DRAIN, 0), (GOT_CORE, 5), (GOT_BESIDE, 10), (GOT_CORE, 4), (RAISE, 1),
+    (GOT_X, 11), (GOT_Y, 8), (RAISE, 0), (GOT_X, 10), (GOT_Y, 9), (OUTER_GRAD, 0), (SUM_SEND, 0),
+    (GOT_Y, 11), (SUM_CORE, 0), (GOT_Y, 10), (SUM_SEND, 1), (SUM_SEND, 2), (GOT_CORE, 8),
+    (SUM_SEND, 3), (GOT_CORE, 9), (GOT_CORE, 11), (GOT_CORE, 10), (RAISED_GRAD, 0), (SUM_CORE, 1),
+    (SUM_CORE, 2), (INNER_GRAD, 0), (SUM_SEND, 4), (SUM_SEND, 5), (SUM_X, 0), (SUM_CORE, 3),
+    (LOWER, 0), (RAISED_GRAD, 1), (SUM_Y, 1), (SUM_CORE, 4), (MIDDLE_GRAD, 0), (SUM_X, 2),
+    (LOWER, 1), (MIDDLE_GRAD, 1), (SUM_Y, 3), (SUM_CORE, 5), (INNER_GRAD, 1), (SUM_SEND, 6),
+    (SUM_Y, 4), (SUM_SEND, 7), (SUM_X, 1), (LOWER, 2), (MIDDLE_NORM, 0), (SUM_X, 3),
+    (SUM_CORE, 6), (OUTPUT_GRAD, 0), (SUM_Y, 5), (ATTENDED_GRAD, 0), (SUM_CORE, 7),
+    (ATTEND_BACK, 0), (SUM_SEND, 8), (SUM_X, 4), (SQUARE_GRAD, 0), (SUM_Y, 6), (SUM_CORE, 8),
+    (SUM_SEND, 9), (SUM_X, 5), (ATTEND_BACK, 1), (SUM_Y, 7), (SQUARE_GRAD, 1), (SUM_CORE, 9),
+    (SUM_X, 6), (SUM_Y, 8), (SUM_SEND, 10), (ATTEND_BACK, 2), (SUM_X, 7), (SUM_CORE, 10),
+    (SQUARE_GRAD, 2), (SUM_SEND, 11), (SUM_Y, 9), (SUM_CORE, 11), (SUM_X, 8), (SUM_Z, 6),
+    (NORMED_GRAD, 1), (SUM_Y, 10), (SUM_Z, 3), (SUM_X, 9), (SUM_Z, 0), (SUM_Y, 11), (SUM_Z, 2),
+    (SUM_Z, 8), (NORMED_GRAD, 0), (SUM_BACK, 6), (SUM_Z, 1), (SUM_X, 10), (SUM_Z, 9), (SUM_Z, 5),
+    (INPUT_GRAD, 0), (SUM_BACK, 0), (SUM_X, 11), (SUM_Z, 4), (SUM_Z, 7), (SUM_DONE, 0),
+    (SMALL, 0), (SUM_BACK, 2), (SUM_Z, 10), (SMALL_SUM, 0), (SUM_BACK, 8), (SUM_BACK, 9),
+    (SUM_BACK, 5), (SUM_Z, 11), (SUM_BACK, 1), (SUM_BACK, 10), (SUM_DONE, 2), (SUM_DONE, 1),
+    (SUM_BACK, 7), (SUM_BACK, 3), (SUM_DONE, 6), (SUM_BACK, 4), (SUM_BACK, 11), (SUM_DONE, 5),
+    (SUM_DONE, 10), (SUM_DONE, 3), (SUM_DONE, 7), (SUM_DONE, 9), (SMALL_DONE, 0), (SUM_DONE, 4),
+    (SUM_DONE, 8), (SUM_DONE, 11),
 )
 
 
@@ -1271,7 +1271,7 @@
             sems((2,)),
         ],
         compiler_params=pltpu.CompilerParams(
-            collective_id=0, has_side_effects=True, vmem_limit_bytes=63 * 2**20
+            collective_id=0, has_side_effects=True, vmem_limit_bytes=127 * 2**19
         ),
     )(length, x, cot, gain_a, gain_f, table, *square, inner, outer)
 

time: 143 us -> 144 us (level)
  no operation moved by 1% of the time
where the time goes in v3:
time: 144 us
  Pallas kernels  142 us (99%)
  between operations  1.48 us (1%)
    pallas_call x1, Pallas kernels, fused_call(): pl.pallas_call(fused_kernel, out_shape=(jax.ShapeDtypeStruct((seq, width)...  137 us
    pallas_call x1, Pallas kernels, finish_call(): pl.pallas_call(finish_kernel, out_shape=[jax.ShapeDtypeStruct(block.shape...  5.42 us

profile of v3, /device:TPU:1, one launch (start us, length us, event | category | flops | bytes accessed | tf_op | source)
XLA Modules:
  0.0 143.7 jit_solution(6852129074724770161)
XLA Ops:
  1.3 136.8 %shard_map.203 = (bf16[512,768]{1,0:T(8,128)(2,1)}, f32[512,768]{1,0:T(8,128)}, bf16[12,96,768]{2,1,0:T(8,128)(2,1)}, f32[8,128]{1,0:T(8,128)}, bf16[6,2,512,512]{3,2,1,0:T(8,128)(2,1)}) custom-call(s32[1]{0:T(128)S(6)} %copy.23.length, bf16[512,768]{1,0:T(8,128)(2,1)} %bitcast.8, bf16[512,768]{1,0:T(8,128)(2,1)} %bitcast.9, bf16[1,96]{1,0:T(2,128)(2,1)} %bitcast.10, ...), custom_call_target="tpu_custom_call" | custom-call | tf_op jit(solution)/shard_map/pallas_call | solution.py:1217
  138.1 5.4 %shard_map.204 = (bf16[512,768]{1,0:T(8,128)(2,1)}, f32[512,768]{1,0:T(8,128)}, f32[96,768]{1,0:T(8,128)}, f32[96,768]{1,0:T(8,128)}, f32[96,768]{1,0:T(8,128)},...) custom-call(bf16[512,768]{1,0:T(8,128)(2,1)} %get-tuple-element.26.b, ...), custom_call_target="tpu_custom_call" | custom-call | tf_op jit(solution)/shard_map/pallas_call | solution.py:1340
